TPU v7x, 128 devices: a whole 4x4x4 slice. The times are simulated.
128 devices in a mesh: gx: 8 (over z, x_hi), gy: 16 (over y, x_lo, core).
Axes of the slice: x: 4 (x_hi: 2, x_lo: 2; x = x_hi * 2 + x_lo), y: 4, z: 4, core: 2. Of those that a mesh axis runs over, the one named last changes fastest.
Arguments:
- intensity: bfloat16 [16, 128, 1024], P(None, 'gy', 'gx'), may hold values from -6 to 6
- first_kernel: bfloat16 [3, 3, 3, 1, 64], replicated, may hold values from -1.25 to 1.25
- second_kernel: bfloat16 [3, 3, 3, 64, 64], replicated, may hold values from -0.21875 to 0.21875
- third_kernel: bfloat16 [3, 3, 3, 64, 64], replicated, may hold values from -0.21875 to 0.21875
- head_weight: bfloat16 [64, 75], replicated, may hold values from -1.5 to 1.5
Outputs:
- affinity: float32 [3, 16, 128, 1024], P(None, None, 'gy', 'gx')
All inputs are finite; a program needn't handle non-finite values.
Results may differ from a plain program's by a relative error of at most 0.00075.
Values may be sent and summed in bfloat16 or wider, within the bound.
A program may use at most 128 MiB of HBM per device.

v0:
```python
import jax
import jax.numpy as jnp
from jax import lax
from jax.sharding import PartitionSpec as P

R = 2


def extended(shard, sides, width):
    for axis, dim in sides:
        devices, length = (lax.axis_size(axis), shard.shape[dim])
        up = [(i, (i + 1) % devices) for i in range(devices - 1)]
        down = [(j, i) for i, j in up]
        last = lax.slice_in_dim(shard, length - width, length, axis=dim)
        initial = lax.slice_in_dim(shard, 0, width, axis=dim)
        before = lax.ppermute(last, axis, up)
        after = lax.ppermute(initial, axis, down)
        shard = jnp.concatenate([before, shard, after], axis=dim)
    return shard


def convolve(volume, kernel):
    return lax.conv_general_dilated(
        volume[None],
        kernel,
        (1, 1, 1),
        [(1, 1), (0, 0), (0, 0)],
        dimension_numbers=("NDHWC", "DHWIO", "NDHWC"),
        preferred_element_type=jnp.float32,
    )[0]


def spread(features):
    return extended(features, (("gx", 2), ("gy", 1)), 1)


def fold_axis(padded, axis, margin, length):
    lower = lax.slice_in_dim(padded, 0, margin, axis=axis)
    middle = lax.slice_in_dim(padded, 2 * margin, 2 * margin + length, axis=axis)
    upper = lax.slice_in_dim(padded, length + 3 * margin, length + 4 * margin, axis=axis)
    widths_low = [(0, 0)] * padded.ndim
    widths_high = [(0, 0)] * padded.ndim
    widths_low[axis] = (0, length - margin)
    widths_high[axis] = (length - margin, 0)
    return middle + jnp.pad(lower, widths_low) + jnp.pad(upper, widths_high)


def coverage(index, tile, count, blending):
    positions = index * tile + jnp.arange(tile)
    sources = positions[:, None] - (jnp.arange(2 * R + 1)[None, :] - R)
    valid = ((sources >= 0) & (sources < tile * count)).astype(jnp.float32)
    return jnp.sum(valid * blending[None, :], axis=1)


def local(intensity, first_kernel, second_kernel, third_kernel, head_weight):
    depth, tile_y, tile_x = intensity.shape
    index_x = lax.axis_index("gx")
    index_y = lax.axis_index("gy")
    tiles_x = lax.axis_size("gx")
    tiles_y = lax.axis_size("gy")
    margin = 1
    padded = extended(intensity, (("gx", 2), ("gy", 1)), margin)
    stem_feat = jax.nn.relu(convolve(padded[..., None], first_kernel)).astype(jnp.bfloat16)
    inner_feat = jax.nn.relu(convolve(spread(stem_feat), second_kernel)).astype(jnp.bfloat16)
    block_feat = jax.nn.relu(
        convolve(spread(inner_feat), third_kernel) + stem_feat.astype(jnp.float32)
    ).astype(jnp.bfloat16)
    window = 2 * R + 1
    blending = (R + 1 - jnp.abs(jnp.arange(window) - R)).astype(jnp.float32)
    logits = jnp.einsum(
        "zyxk,ko->ozyx", block_feat, head_weight, preferred_element_type=jnp.float32
    )
    weighted = jax.nn.sigmoid(logits).reshape(window, window, 3, depth, tile_y, tile_x)
    weighted = weighted * (blending[:, None] * blending[None, :])[:, :, None, None, None, None]
    canvas = jnp.zeros((3, depth, tile_y + 2 * R, tile_x + 2 * R), jnp.float32)
    for offset_x in range(window):
        for offset_y in range(window):
            canvas = canvas.at[
                :, :, offset_y : offset_y + tile_y, offset_x : offset_x + tile_x
            ].add(weighted[offset_x, offset_y])
    beside_all = extended(canvas, (("gx", 3), ("gy", 2)), R)
    numerator = fold_axis(fold_axis(beside_all, 3, R, tile_x), 2, R, tile_y)
    weight_total = (
        coverage(index_y, tile_y, tiles_y, blending)[:, None]
        * coverage(index_x, tile_x, tiles_x, blending)[None, :]
    )
    return numerator / weight_total[None, None, :, :]


def solution(mesh):
    in_specs = (P(None, "gy", "gx"), P(), P(), P(), P())
    out_specs = P(None, None, "gy", "gx")
    return jax.shard_map(local, mesh=mesh, in_specs=in_specs, out_specs=out_specs, check_vma=False)
```

profile of v0, /device:TPU:1, one launch (start us, length us, event | category | flops | bytes accessed | tf_op | source)
XLA Modules:
  0.0 594.0 jit_solution(17001828529746968971)
XLA Ops:
  0.9 5.5 collective-permute-start
  9.0 3.6 collective-permute-done.1
  13.5 4.2 collective-permute-start.2
  26.9 15.1 %maximum_convert_fusion.1 = bf16[16,8,8,17,64]{4,2,3,1,0:T(8,128)(2,1)S(1)} fusion(pred[8,17]{0,1:T(8,128)(4,1)} %constant.804, bf16[16,10,8,19,1]{2,4,3,1,0:T(2,128)(2,1)S(1)} %copy.48, bf16[3,3,3,1,64]{4,2,3,1,0:T(4,128)(2,1)} %param.56), kind=kOutput, calls=%fused_computation.4 | convolution fusion | flops 60997632 | bytes 2280456 | tf_op jit(solution)/shard_map/conv_general_dilated | solution.py:23
  46.3 5.9 collective-permute-start.4
  53.5 4.8 collective-permute-done.5
  58.4 5.8 pad_maximum_fusion.5
  68.4 14.3 %collective-permute-start.7 = (bf16[16,1,130,64]{2,3,1,0:T(8,128)(2,1)S(1)}, bf16[16,1,130,64]{2,3,1,0:T(8,128)(2,1)}, u32[]{:S(2)}, u32[]{:S(2)}) collective-permute-start(bf16[16,1,130,64]{2,3,1,0:T(8,128)(2,1)S(1)} %copy.52), channel_id=1, source_target_pairs={{1,0},{2,1},{3,2},{4,3},{5,4},{6,5},{7,6},{8,7},{9,8},{10,9},{11,1... | collective-permute-start | bytes 798728 | tf_op jit(solution)/shard_map/ppermute | solution.py:17
  87.4 9.3 %maximum_bitcast_fusion = bf16[16,10,1,130,64]{4,1,3,0,2:T(8,128)(2,1)} fusion(bf16[16,1,130,64]{3,1,2,0:T(2,128)(2,1)S(1)} %copy.54, bf16[16,8,1,64]{3,1,2,0:T(8,128)(2,1)S(1)} %collective-permute-done.5, bf16[16,8,128,64]{3,1,2,0:T(8,128)(2,1)} %copy-done.2, bf16[16,8,1,64]{3,1,2,0:T(8,128)(2,1)S(1)} %collective-permute-done.4, ...), kind=kLoop, calls=%fused_computation.5 | loop fusion | flops 13312000 | bytes 5324800 | tf_op jit(solution)/shard_map/broadcast_in_dim | solution.py:24
  96.7 9.3 %pad.123 = bf16[16,10,1,136,64]{4,1,3,0,2:T(8,128)(2,1)} pad(bf16[16,10,1,130,64]{4,1,3,0,2:T(8,128)(2,1)} %maximum_bitcast_fusion, bf16[]{:T(256)} %constant.792), padding=0_0x0_0x0_0x0_6x0_0 | pad | bytes 5447682 | tf_op jit(solution)/shard_map/broadcast_in_dim | solution.py:24
  106.0 5.0 copy.57
  111.2 16.8 %maximum_convert_fusion = bf16[16,8,8,17,64]{4,2,3,1,0:T(8,128)(2,1)S(1)} fusion(pred[8,17]{0,1:T(8,128)(4,1)S(1)} %copy-done.11, bf16[3,3,3,64,64]{4,3,2,1,0:T(8,128)(2,1)S(1)} %copy-done, bf16[16,10,1,7,2,64]{5,3,4,1,0,2:T(8,128)(2,1)S(1)} %slice.1095, bf16[16,10,1,8,17,64]{5,3,4,1,0,2:T(8,128)(2,1)S(1)} %copy.57), kind=kOutput, calls=%fused_computation.3 | convolution fusion | flops 3702620160 | bytes 5521544 | tf_op jit(solution)/shard_map/conv_general_dilated | solution.py:23
  131.2 4.4 collective-permute-start.8
  137.5 4.3 collective-permute-done.9
  141.8 5.8 pad_maximum_fusion.2
  148.3 4.7 collective-permute-start.10
  155.8 3.3 collective-permute-done.10
  160.6 8.3 %collective-permute-done.11 = bf16[16,1,130,64]{2,3,1,0:T(8,128)(2,1)} collective-permute-done((bf16[16,1,130,64]{2,3,1,0:T(8,128)(2,1)S(1)}, bf16[16,1,130,64]{2,3,1,0:T(8,128)(2,1)}, u32[]{:S(2)}, u32[]{:S(2)}) %collective-permute-start.11) | collective-permute-done | bytes 266272 | tf_op jit(solution)/shard_map/ppermute | solution.py:17
  171.6 9.3 %maximum_bitcast_fusion.1 = bf16[16,10,1,130,64]{4,1,3,0,2:T(8,128)(2,1)} fusion(bf16[16,1,130,64]{3,1,2,0:T(2,128)(2,1)S(1)} %copy.62, bf16[16,8,1,64]{3,1,2,0:T(8,128)(2,1)S(1)} %collective-permute-done.9, bf16[16,8,128,64]{3,1,2,0:T(8,128)(2,1)} %copy-done.3, bf16[16,8,1,64]{3,1,2,0:T(8,128)(2,1)S(1)} %collective-permute-done.8, ...), kind=kLoop, calls=%fused_computation.6 | loop fusion | flops 13312000 | bytes 5324800 | tf_op jit(solution)/shard_map/broadcast_in_dim | solution.py:24
  180.9 9.3 %pad.125 = bf16[16,10,1,136,64]{4,1,3,0,2:T(8,128)(2,1)} pad(bf16[16,10,1,130,64]{4,1,3,0,2:T(8,128)(2,1)} %maximum_bitcast_fusion.1, bf16[]{:T(256)} %constant.792), padding=0_0x0_0x0_0x0_6x0_0 | pad | bytes 5447682 | tf_op jit(solution)/shard_map/broadcast_in_dim | solution.py:24
  190.1 5.0 copy.65
  195.4 18.9 %broadcast_select_fusion = f32[16,8,8,17,64]{4,2,3,1,0:T(8,128)} fusion(pred[8,17]{0,1:T(8,128)(4,1)S(1)} %copy-done.11, bf16[3,3,3,64,64]{4,3,2,1,0:T(8,128)(2,1)S(1)} %copy-done.9, bf16[16,10,1,7,2,64]{5,3,4,1,0,2:T(8,128)(2,1)S(1)} %slice.1099, bf16[16,10,1,8,17,64]{5,3,4,1,0,2:T(8,128)(2,1)S(1)} %copy.65), kind=kOutput, calls=%fused_computation.24 | convolution fusion | flops 3700391936 | bytes 7749768 | tf_op jit(solution)/shard_map/conv_general_dilated | solution.py:23
  214.3 5.1 copy.66
  238.8 15.6 %scatter-add.91 = f32[3,16,12,132]{3,2,1,0:T(8,128)S(1)} dynamic-update-slice(f32[3,16,12,132]{3,2,1,0:T(8,128)S(1)} %scatter-add.90, f32[3,16,8,128]{3,2,1,0:T(8,128)S(1)} %fusion.54, s32[]{:T(128)} %constant.770.clone.1, s32[]{:T(128)} %constant.770.clone.1, s32[]{:T(128)} %bitcast.27, s32[]{:T(128)} %bitcast.28) | dynamic-update-slice | bytes 393220 | tf_op jit(solution)/shard_map/scatter-add | solution.py:80
  255.5 14.4 %scatter-add.94 = f32[3,16,12,132]{3,2,1,0:T(8,128)S(1)} dynamic-update-slice(f32[3,16,12,132]{3,2,1,0:T(8,128)S(1)} %scatter-add.91, f32[3,16,8,128]{3,2,1,0:T(8,128)S(1)} %fusion.53, s32[]{:T(128)} %constant.770.clone.1, s32[]{:T(128)} %constant.770.clone.1, s32[]{:T(128)} %constant.771.clone.1, s32[]{:T(128)} %constant.771.clone.1) | dynamic-update-slice | bytes 393220 | tf_op jit(solution)/shard_map/scatter-add | solution.py:80
  271.0 14.4 %scatter-add.95 = f32[3,16,12,132]{3,2,1,0:T(8,128)S(1)} dynamic-update-slice(f32[3,16,12,132]{3,2,1,0:T(8,128)S(1)} %scatter-add.94, f32[3,16,8,128]{3,2,1,0:T(8,128)S(1)} %fusion.52, s32[]{:T(128)} %constant.770.clone.1, s32[]{:T(128)} %constant.770.clone.1, s32[]{:T(128)} %constant.772.clone.1, s32[]{:T(128)} %constant.771.clone.1) | dynamic-update-slice | bytes 393220 | tf_op jit(solution)/shard_map/scatter-add | solution.py:80
  286.5 14.4 %scatter-add.96 = f32[3,16,12,132]{3,2,1,0:T(8,128)S(1)} dynamic-update-slice(f32[3,16,12,132]{3,2,1,0:T(8,128)S(1)} %scatter-add.95, f32[3,16,8,128]{3,2,1,0:T(8,128)S(1)} %fusion.51, s32[]{:T(128)} %constant.770.clone.1, s32[]{:T(128)} %constant.770.clone.1, s32[]{:T(128)} %constant.768.clone.1, s32[]{:T(128)} %constant.771.clone.1) | dynamic-update-slice | bytes 393220 | tf_op jit(solution)/shard_map/scatter-add | solution.py:80
  302.0 14.4 %scatter-add.99 = f32[3,16,12,132]{3,2,1,0:T(8,128)S(1)} dynamic-update-slice(f32[3,16,12,132]{3,2,1,0:T(8,128)S(1)} %scatter-add.96, f32[3,16,8,128]{3,2,1,0:T(8,128)S(1)} %fusion.50, s32[]{:T(128)} %constant.770.clone.1, s32[]{:T(128)} %constant.770.clone.1, s32[]{:T(128)} %constant.773.clone.1, s32[]{:T(128)} %constant.771.clone.1) | dynamic-update-slice | bytes 393220 | tf_op jit(solution)/shard_map/scatter-add | solution.py:80
  319.4 15.8 %scatter-add.100 = f32[3,16,12,132]{3,2,1,0:T(8,128)S(1)} dynamic-update-slice(f32[3,16,12,132]{3,2,1,0:T(8,128)S(1)} %scatter-add.99, f32[3,16,8,128]{3,2,1,0:T(8,128)S(1)} %add_select_fusion.2, s32[]{:T(128)} %constant.770.clone.1, s32[]{:T(128)} %constant.770.clone.1, s32[]{:T(128)} %bitcast.34, s32[]{:T(128)} %bitcast.35) | dynamic-update-slice | bytes 393220 | tf_op jit(solution)/shard_map/scatter-add | solution.py:80
  336.2 14.4 %scatter-add.101 = f32[3,16,12,132]{3,2,1,0:T(8,128)S(1)} dynamic-update-slice(f32[3,16,12,132]{3,2,1,0:T(8,128)S(1)} %scatter-add.100, f32[3,16,8,128]{3,2,1,0:T(8,128)S(1)} %fusion.49, s32[]{:T(128)} %constant.770.clone.1, s32[]{:T(128)} %constant.770.clone.1, s32[]{:T(128)} %constant.771.clone.1, s32[]{:T(128)} %constant.772.clone.1) | dynamic-update-slice | bytes 393220 | tf_op jit(solution)/shard_map/scatter-add | solution.py:80
  351.7 14.4 %scatter-add.104 = f32[3,16,12,132]{3,2,1,0:T(8,128)S(1)} dynamic-update-slice(f32[3,16,12,132]{3,2,1,0:T(8,128)S(1)} %scatter-add.101, f32[3,16,8,128]{3,2,1,0:T(8,128)S(1)} %fusion.48, s32[]{:T(128)} %constant.770.clone.1, s32[]{:T(128)} %constant.770.clone.1, s32[]{:T(128)} %constant.772.clone.1, s32[]{:T(128)} %constant.772.clone.1) | dynamic-update-slice | bytes 393220 | tf_op jit(solution)/shard_map/scatter-add | solution.py:80
  367.2 14.4 %scatter-add.105 = f32[3,16,12,132]{3,2,1,0:T(8,128)S(1)} dynamic-update-slice(f32[3,16,12,132]{3,2,1,0:T(8,128)S(1)} %scatter-add.104, f32[3,16,8,128]{3,2,1,0:T(8,128)S(1)} %fusion.47, s32[]{:T(128)} %constant.770.clone.1, s32[]{:T(128)} %constant.770.clone.1, s32[]{:T(128)} %constant.768.clone.1, s32[]{:T(128)} %constant.772.clone.1) | dynamic-update-slice | bytes 393220 | tf_op jit(solution)/shard_map/scatter-add | solution.py:80
  382.7 14.4 %scatter-add.106 = f32[3,16,12,132]{3,2,1,0:T(8,128)S(1)} dynamic-update-slice(f32[3,16,12,132]{3,2,1,0:T(8,128)S(1)} %scatter-add.105, f32[3,16,8,128]{3,2,1,0:T(8,128)S(1)} %fusion.46, s32[]{:T(128)} %constant.770.clone.1, s32[]{:T(128)} %constant.770.clone.1, s32[]{:T(128)} %constant.773.clone.1, s32[]{:T(128)} %constant.772.clone.1) | dynamic-update-slice | bytes 393220 | tf_op jit(solution)/shard_map/scatter-add | solution.py:80
  400.1 15.8 %scatter-add.109 = f32[3,16,12,132]{3,2,1,0:T(8,128)S(1)} dynamic-update-slice(f32[3,16,12,132]{3,2,1,0:T(8,128)S(1)} %scatter-add.106, f32[3,16,8,128]{3,2,1,0:T(8,128)S(1)} %add_select_fusion.1, s32[]{:T(128)} %constant.770.clone.1, s32[]{:T(128)} %constant.770.clone.1, s32[]{:T(128)} %bitcast.41, s32[]{:T(128)} %bitcast.42) | dynamic-update-slice | bytes 393220 | tf_op jit(solution)/shard_map/scatter-add | solution.py:80
  417.0 14.4 %scatter-add.110 = f32[3,16,12,132]{3,2,1,0:T(8,128)S(1)} dynamic-update-slice(f32[3,16,12,132]{3,2,1,0:T(8,128)S(1)} %scatter-add.109, f32[3,16,8,128]{3,2,1,0:T(8,128)S(1)} %fusion.45, s32[]{:T(128)} %constant.770.clone.1, s32[]{:T(128)} %constant.770.clone.1, s32[]{:T(128)} %constant.771.clone.1, s32[]{:T(128)} %constant.768.clone.1) | dynamic-update-slice | bytes 393220 | tf_op jit(solution)/shard_map/scatter-add | solution.py:80
  432.5 14.4 %scatter-add.111 = f32[3,16,12,132]{3,2,1,0:T(8,128)S(1)} dynamic-update-slice(f32[3,16,12,132]{3,2,1,0:T(8,128)S(1)} %scatter-add.110, f32[3,16,8,128]{3,2,1,0:T(8,128)S(1)} %fusion.44, s32[]{:T(128)} %constant.770.clone.1, s32[]{:T(128)} %constant.770.clone.1, s32[]{:T(128)} %constant.772.clone.1, s32[]{:T(128)} %constant.768.clone.1) | dynamic-update-slice | bytes 393220 | tf_op jit(solution)/shard_map/scatter-add | solution.py:80
  448.0 14.4 %scatter-add.114 = f32[3,16,12,132]{3,2,1,0:T(8,128)S(1)} dynamic-update-slice(f32[3,16,12,132]{3,2,1,0:T(8,128)S(1)} %scatter-add.111, f32[3,16,8,128]{3,2,1,0:T(8,128)S(1)} %fusion.43, s32[]{:T(128)} %constant.770.clone.1, s32[]{:T(128)} %constant.770.clone.1, s32[]{:T(128)} %constant.768.clone.1, s32[]{:T(128)} %constant.768.clone.1) | dynamic-update-slice | bytes 393220 | tf_op jit(solution)/shard_map/scatter-add | solution.py:80
  463.5 14.4 %scatter-add.115 = f32[3,16,12,132]{3,2,1,0:T(8,128)S(1)} dynamic-update-slice(f32[3,16,12,132]{3,2,1,0:T(8,128)S(1)} %scatter-add.114, f32[3,16,8,128]{3,2,1,0:T(8,128)S(1)} %fusion.42, s32[]{:T(128)} %constant.770.clone.1, s32[]{:T(128)} %constant.770.clone.1, s32[]{:T(128)} %constant.773.clone.1, s32[]{:T(128)} %constant.768.clone.1) | dynamic-update-slice | bytes 393220 | tf_op jit(solution)/shard_map/scatter-add | solution.py:80
  480.8 15.7 %scatter-add.116 = f32[3,16,12,132]{3,2,1,0:T(8,128)S(1)} dynamic-update-slice(f32[3,16,12,132]{3,2,1,0:T(8,128)S(1)} %scatter-add.115, f32[3,16,8,128]{3,2,1,0:T(8,128)S(1)} %add_select_fusion, s32[]{:T(128)} %constant.770.clone.1, s32[]{:T(128)} %constant.770.clone.1, s32[]{:T(128)} %bitcast.48, s32[]{:T(128)} %bitcast.49) | dynamic-update-slice | bytes 393220 | tf_op jit(solution)/shard_map/scatter-add | solution.py:80
  497.6 14.4 %scatter-add.119 = f32[3,16,12,132]{3,2,1,0:T(8,128)S(1)} dynamic-update-slice(f32[3,16,12,132]{3,2,1,0:T(8,128)S(1)} %scatter-add.116, f32[3,16,8,128]{3,2,1,0:T(8,128)S(1)} %fusion.41, s32[]{:T(128)} %constant.770.clone.1, s32[]{:T(128)} %constant.770.clone.1, s32[]{:T(128)} %constant.771.clone.1, s32[]{:T(128)} %constant.773.clone.1) | dynamic-update-slice | bytes 393220 | tf_op jit(solution)/shard_map/scatter-add | solution.py:80
  513.1 14.7 %scatter-add.120 = f32[3,16,12,132]{3,2,1,0:T(8,128)S(1)} dynamic-update-slice(f32[3,16,12,132]{3,2,1,0:T(8,128)S(1)} %scatter-add.119, f32[3,16,8,128]{3,2,1,0:T(8,128)S(1)} %fusion.40, s32[]{:T(128)} %constant.770.clone.1, s32[]{:T(128)} %constant.770.clone.1, s32[]{:T(128)} %constant.772.clone.1, s32[]{:T(128)} %constant.773.clone.1) | dynamic-update-slice | bytes 393220 | tf_op jit(solution)/shard_map/scatter-add | solution.py:80
  528.8 14.4 %scatter-add.121 = f32[3,16,12,132]{3,2,1,0:T(8,128)S(1)} dynamic-update-slice(f32[3,16,12,132]{3,2,1,0:T(8,128)S(1)} %scatter-add.120, f32[3,16,8,128]{3,2,1,0:T(8,128)S(1)} %fusion.39, s32[]{:T(128)} %constant.770.clone.1, s32[]{:T(128)} %constant.770.clone.1, s32[]{:T(128)} %constant.768.clone.1, s32[]{:T(128)} %constant.773.clone.1) | dynamic-update-slice | bytes 393220 | tf_op jit(solution)/shard_map/scatter-add | solution.py:80
  544.3 14.4 %scatter-add.124 = f32[3,16,12,132]{3,2,1,0:T(8,128)S(1)} dynamic-update-slice(f32[3,16,12,132]{3,2,1,0:T(8,128)S(1)} %scatter-add.121, f32[3,16,8,128]{3,2,1,0:T(8,128)S(1)} %fusion.38, s32[]{:T(128)} %constant.770.clone.1, s32[]{:T(128)} %constant.770.clone.1, s32[]{:T(128)} %constant.773.clone.1, s32[]{:T(128)} %constant.773.clone.1) | dynamic-update-slice | bytes 393220 | tf_op jit(solution)/shard_map/scatter-add | solution.py:80
  558.9 4.7 collective-permute-start.12
  565.2 3.2 collective-permute-done.12
  568.4 6.2 %collective-permute-done.13 = f32[3,16,12,2]{3,2,1,0:T(8,128)S(1)} collective-permute-done((f32[3,16,12,2]{3,2,1,0:T(8,128)S(1)}, f32[3,16,12,2]{3,2,1,0:T(8,128)S(1)}, u32[]{:S(2)}, u32[]{:S(2)}) %collective-permute-start.13) | collective-permute-done | bytes 4640 | tf_op jit(solution)/shard_map/ppermute | solution.py:17
  574.9 10.9 %collective-permute-start.14 = (f32[3,16,2,136]{3,2,1,0:T(2,128)S(1)}, f32[3,16,2,136]{3,2,1,0:T(2,128)S(1)}, u32[]{:S(2)}, u32[]{:S(2)}) collective-permute-start(f32[3,16,2,136]{3,2,1,0:T(2,128)S(1)} %get-tuple-element.315), channel_id=1, source_target_pairs={{0,1},{1,2},{2,3},{3,4},{4,5},{5,6},{6,7},{7,8},{8,9},{9,10},{10,1... | collective-permute-start | bytes 156680 | tf_op jit(solution)/shard_map/ppermute | solution.py:16
  587.9 3.9 collective-permute-done.15
  (126 shorter events, 91.8 us)
Async XLA Ops:
  0.0 111.2 %copy-start = (bf16[3,3,3,64,64]{4,3,2,1,0:T(8,128)(2,1)S(1)}, bf16[3,3,3,64,64]{4,3,2,1,0:T(8,128)(2,1)}, u32[]{:S(2)}) copy-start(bf16[3,3,3,64,64]{4,3,2,1,0:T(8,128)(2,1)} %param.57) | copy-start | bytes 663556
  0.9 8.0 %collective-permute-start = (bf16[16,8,1]{2,1,0:T(8,128)(2,1)S(1)}, bf16[16,8,1]{2,1,0:T(8,128)(2,1)S(1)}, u32[]{:S(2)}, u32[]{:S(2)}) collective-permute-start(bf16[16,8,1]{2,1,0:T(8,128)(2,1)S(1)} %get-tuple-element.321), channel_id=1, source_target_pairs={{0,16},{16,32},{32,48},{48,64},{64,80},{80,96},{96,112},{1,17},{17... | collective-permute-start | bytes 776 | tf_op jit(solution)/shard_map/ppermute | solution.py:16
  6.4 6.2 %collective-permute-start.1 = (bf16[16,8,1]{2,1,0:T(8,128)(2,1)S(1)}, bf16[16,8,1]{2,1,0:T(8,128)(2,1)S(1)}, u32[]{:S(2)}, u32[]{:S(2)}) collective-permute-start(bf16[16,8,1]{2,1,0:T(8,128)(2,1)S(1)} %get-tuple-element.322), channel_id=1, source_target_pairs={{16,0},{32,16},{48,32},{64,48},{80,64},{96,80},{112,96},{17,1},{33... | collective-permute-start | bytes 776 | tf_op jit(solution)/shard_map/ppermute | solution.py:17
  13.5 6.8 %collective-permute-start.2 = (bf16[16,1,130]{2,1,0:T(2,128)(2,1)S(1)}, bf16[16,1,130]{2,1,0:T(2,128)(2,1)S(1)}, u32[]{:S(2)}, u32[]{:S(2)}) collective-permute-start(bf16[16,1,130]{2,1,0:T(2,128)(2,1)S(1)} %get-tuple-element.319), channel_id=1, source_target_pairs={{0,1},{1,2},{2,3},{3,4},{4,5},{5,6},{6,7},{7,8},{8,9},{9,10},{10,1... | collective-permute-start | bytes 12488 | tf_op jit(solution)/shard_map/ppermute | solution.py:16
  17.7 5.1 collective-permute-start.3
  42.9 3.4 copy-start.4
  43.2 2.2 copy-start.2
  45.4 37.3 %copy-start.7 = (s32[4]{0:T(128)S(1)}, s32[4]{0:T(128)}, u32[]{:S(2)}) copy-start(s32[4]{0:T(128)} %constant.775.clone.1) | copy-start | bytes 52
  46.3 7.2 %collective-permute-start.4 = (bf16[16,8,1,64]{3,1,2,0:T(8,128)(2,1)S(1)}, bf16[16,8,1,64]{3,1,2,0:T(8,128)(2,1)S(1)}, u32[]{:S(2)}, u32[]{:S(2)}) collective-permute-start(bf16[16,8,1,64]{3,1,2,0:T(8,128)(2,1)S(1)} %get-tuple-element.313), channel_id=1, source_target_pairs={{0,16},{16,32},{32,48},{48,64},{64,80},{80,96},{96,112},{1,17},{17... | collective-permute-start | bytes 49160 | tf_op jit(solution)/shard_map/ppermute | solution.py:16
  52.2 6.2 %collective-permute-start.5 = (bf16[16,8,1,64]{3,1,2,0:T(8,128)(2,1)S(1)}, bf16[16,8,1,64]{3,1,2,0:T(8,128)(2,1)S(1)}, u32[]{:S(2)}, u32[]{:S(2)}) collective-permute-start(bf16[16,8,1,64]{3,1,2,0:T(8,128)(2,1)S(1)} %get-tuple-element.314), channel_id=1, source_target_pairs={{16,0},{32,16},{48,32},{64,48},{80,64},{96,80},{112,96},{17,1},{33... | collective-permute-start | bytes 49160 | tf_op jit(solution)/shard_map/ppermute | solution.py:17
  64.9 18.7 %collective-permute-start.6 = (bf16[16,1,130,64]{2,3,1,0:T(8,128)(2,1)S(1)}, bf16[16,1,130,64]{2,3,1,0:T(8,128)(2,1)S(1)}, u32[]{:S(2)}, u32[]{:S(2)}) collective-permute-start(bf16[16,1,130,64]{2,3,1,0:T(8,128)(2,1)S(1)} %copy.51), channel_id=1, source_target_pairs={{0,1},{1,2},{2,3},{3,4},{4,5},{5,6},{6,7},{7,8},{8,9},{9,10},{10,1... | collective-permute-start | bytes 798728 | tf_op jit(solution)/shard_map/ppermute | solution.py:16
  68.4 16.4 %collective-permute-start.7 = (bf16[16,1,130,64]{2,3,1,0:T(8,128)(2,1)S(1)}, bf16[16,1,130,64]{2,3,1,0:T(8,128)(2,1)}, u32[]{:S(2)}, u32[]{:S(2)}) collective-permute-start(bf16[16,1,130,64]{2,3,1,0:T(8,128)(2,1)S(1)} %copy.52), channel_id=1, source_target_pairs={{1,0},{2,1},{3,2},{4,3},{5,4},{6,5},{7,6},{8,7},{9,8},{10,9},{11,1... | collective-permute-start | bytes 798728 | tf_op jit(solution)/shard_map/ppermute | solution.py:17
  106.0 5.2 copy-start.11
  129.2 2.0 copy-start.3
  131.2 6.3 %collective-permute-start.8 = (bf16[16,8,1,64]{3,1,2,0:T(8,128)(2,1)S(1)}, bf16[16,8,1,64]{3,1,2,0:T(8,128)(2,1)S(1)}, u32[]{:S(2)}, u32[]{:S(2)}) collective-permute-start(bf16[16,8,1,64]{3,1,2,0:T(8,128)(2,1)S(1)} %get-tuple-element.311), channel_id=1, source_target_pairs={{0,16},{16,32},{32,48},{48,64},{64,80},{80,96},{96,112},{1,17},{17... | collective-permute-start | bytes 49160 | tf_op jit(solution)/shard_map/ppermute | solution.py:16
  135.6 6.2 %collective-permute-start.9 = (bf16[16,8,1,64]{3,1,2,0:T(8,128)(2,1)S(1)}, bf16[16,8,1,64]{3,1,2,0:T(8,128)(2,1)S(1)}, u32[]{:S(2)}, u32[]{:S(2)}) collective-permute-start(bf16[16,8,1,64]{3,1,2,0:T(8,128)(2,1)S(1)} %get-tuple-element.312), channel_id=1, source_target_pairs={{16,0},{32,16},{48,32},{64,48},{80,64},{96,80},{112,96},{17,1},{33... | collective-permute-start | bytes 49160 | tf_op jit(solution)/shard_map/ppermute | solution.py:17
  148.3 10.8 %collective-permute-start.10 = (bf16[16,1,130,64]{2,3,1,0:T(8,128)(2,1)S(1)}, bf16[16,1,130,64]{2,3,1,0:T(8,128)(2,1)S(1)}, u32[]{:S(2)}, u32[]{:S(2)}) collective-permute-start(bf16[16,1,130,64]{2,3,1,0:T(8,128)(2,1)S(1)} %copy.59), channel_id=1, source_target_pairs={{0,1},{1,2},{2,3},{3,4},{4,5},{5,6},{6,7},{7,8},{8,9},{9,10},{10,1... | collective-permute-start | bytes 798728 | tf_op jit(solution)/shard_map/ppermute | solution.py:16
  153.8 15.2 %collective-permute-start.11 = (bf16[16,1,130,64]{2,3,1,0:T(8,128)(2,1)S(1)}, bf16[16,1,130,64]{2,3,1,0:T(8,128)(2,1)}, u32[]{:S(2)}, u32[]{:S(2)}) collective-permute-start(bf16[16,1,130,64]{2,3,1,0:T(8,128)(2,1)S(1)} %copy.60), channel_id=1, source_target_pairs={{1,0},{2,1},{3,2},{4,3},{5,4},{6,5},{7,6},{8,7},{9,8},{10,9},{11,1... | collective-permute-start | bytes 798728 | tf_op jit(solution)/shard_map/ppermute | solution.py:17
  190.1 5.2 copy-start.9
  190.1 29.2 %slice-start = ((s8[4456448]{0:T(1024)(128)(4,1)}), s8[262144]{0:T(1024)(128)(4,1)S(1)}, s32[]{:S(2)}) async-start(s8[4456448]{0:T(1024)(128)(4,1)} %bitcast.163), calls=%async_computation | async-start | bytes 524288
  195.4 24.0 %slice-start.1 = ((s8[4456448]{0:T(1024)(128)(4,1)}), s8[4194304]{0:T(1024)(128)(4,1)S(1)}, s32[]{:S(2)}) async-start(s8[4456448]{0:T(1024)(128)(4,1)} %bitcast.163), calls=%async_computation.1 | async-start | bytes 8388608
  219.4 1.2 copy-start.10
  225.3 2.2 copy-start.5
  512.0 80.4 %copy-start.6 = (pred[128]{0:T(512)(128)(4,1)S(1)}, pred[128]{0:T(512)(128)(4,1)}, u32[]{:S(2)}) copy-start(pred[128]{0:T(512)(128)(4,1)} %constant.777.clone.1) | copy-start | bytes 388
  528.8 63.9 %copy-start.8 = (pred[8]{0:T(512)(128)(4,1)S(1)}, pred[8]{0:T(512)(128)(4,1)}, u32[]{:S(2)}) copy-start(pred[8]{0:T(512)(128)(4,1)} %constant.778.clone.1) | copy-start | bytes 28
  528.8 64.7 %copy-start.1 = (bf16[3,3,3,64,64]{4,3,2,1,0:T(8,128)(2,1)S(1)}, bf16[3,3,3,64,64]{4,3,2,1,0:T(8,128)(2,1)}, u32[]{:S(2)}) copy-start(bf16[3,3,3,64,64]{4,3,2,1,0:T(8,128)(2,1)} %param.57) | copy-start | bytes 663556
  558.9 9.4 %collective-permute-start.12 = (f32[3,16,12,2]{3,2,1,0:T(8,128)S(1)}, f32[3,16,12,2]{3,2,1,0:T(8,128)S(1)}, u32[]{:S(2)}, u32[]{:S(2)}) collective-permute-start(f32[3,16,12,2]{3,2,1,0:T(8,128)S(1)} %get-tuple-element.317), channel_id=1, source_target_pairs={{0,16},{16,32},{32,48},{48,64},{64,80},{80,96},{96,112},{1,17},{17... | collective-permute-start | bytes 13832 | tf_op jit(solution)/shard_map/ppermute | solution.py:16
  563.7 10.9 %collective-permute-start.13 = (f32[3,16,12,2]{3,2,1,0:T(8,128)S(1)}, f32[3,16,12,2]{3,2,1,0:T(8,128)S(1)}, u32[]{:S(2)}, u32[]{:S(2)}) collective-permute-start(f32[3,16,12,2]{3,2,1,0:T(8,128)S(1)} %get-tuple-element.318), channel_id=1, source_target_pairs={{16,0},{32,16},{48,32},{64,48},{80,64},{96,80},{112,96},{17,1},{33... | collective-permute-start | bytes 13832 | tf_op jit(solution)/shard_map/ppermute | solution.py:17
  574.9 12.9 %collective-permute-start.14 = (f32[3,16,2,136]{3,2,1,0:T(2,128)S(1)}, f32[3,16,2,136]{3,2,1,0:T(2,128)S(1)}, u32[]{:S(2)}, u32[]{:S(2)}) collective-permute-start(f32[3,16,2,136]{3,2,1,0:T(2,128)S(1)} %get-tuple-element.315), channel_id=1, source_target_pairs={{0,1},{1,2},{2,3},{3,4},{4,5},{5,6},{6,7},{7,8},{8,9},{9,10},{10,1... | collective-permute-start | bytes 156680 | tf_op jit(solution)/shard_map/ppermute | solution.py:16
  585.8 5.9 collective-permute-start.15
where the time goes:
time: 605 us; the launch traced here: 594 us
  local copies, waits for them, and re-layouts  363 us (60%)
  starting transfers between devices  68.2 us (11%)
  other arithmetic  68.1 us (11%)
  matrix products  53 us (9%)
  waiting for transfers between devices  40.2 us (7%)
    scatter-add x25, local copies, waits for them, and re-layouts, local(): canvas = canvas.at[:, :, offset_y:offset_y + tile_y, offset_x:offset_x +...  300 us
    conv_general_dilated x3, matrix products, convolve(): lax.conv_general_dilated(volume[None], kernel, (1, 1, 1), [(1, 1), (0, 0)...  50.8 us
    ppermute x8, starting transfers between devices, extended(): before = lax.ppermute(last, axis, up)  43 us
    ppermute x8, waiting for transfers between devices, extended(): after = lax.ppermute(initial, axis, down)  33.6 us
    ppermute x8, starting transfers between devices, extended(): after = lax.ppermute(initial, axis, down)  25.2 us
    add x21, other arithmetic, local(): canvas = canvas.at[:, :, offset_y:offset_y + tile_y, offset_x:offset_x +...  21.9 us
    broadcast_in_dim x2, local copies, waits for them, and re-layouts, convolve(): volume[None]  18.6 us
    broadcast_in_dim x2, other arithmetic, convolve(): volume[None]  18.5 us
  transfers between devices with their start and end apart: 16, of which 9 were waited for; matrix products, arithmetic and copies ran while one was open for 1% of the time, Pallas kernels for 0%

commit v1 on v0

v1 whole, which is shorter than its diff:
```python
import functools

import jax
import jax.numpy as jnp
import numpy as np
from jax import lax
from jax.experimental import pallas as pl
from jax.experimental.pallas import tpu as pltpu
from jax.sharding import PartitionSpec as P

R = 2
C = 64
Z = 16
TY = 8
TX = 128
BF = jnp.bfloat16
F32 = jnp.float32
MESH = pl.DeviceIdType.MESH

STEM_PAIRS = 8
INNER_PAIRS = 7
BLOCK_PAIRS = 6
STEM_X = 68
INNER_X = 67
BLOCK_X = 66
XT = 17


def exchange_kernel(tile_ref, out_ref, send_sem, recv_sem, local_sem):
    gx, gy = lax.axis_index("gx"), lax.axis_index("gy")
    nx, ny = lax.axis_size("gx"), lax.axis_size("gy")
    around = [(dy, dx) for dy in (-1, 0, 1) for dx in (-1, 0, 1) if (dy, dx) != (0, 0)]

    def device(dy, dx):
        return (lax.rem(gx + dx + nx, nx), lax.rem(gy + dy + ny, ny))

    barrier = pltpu.get_barrier_semaphore()
    for dy, dx in around:
        pl.semaphore_signal(barrier, inc=1, device_id=device(dy, dx), device_id_type=MESH)
    own = pltpu.make_async_copy(tile_ref, out_ref.at[4], local_sem)
    own.start()
    pl.semaphore_wait(barrier, len(around))
    copies = []
    for n, (dy, dx) in enumerate(around):
        slot = (1 - dy) * 3 + (1 - dx)
        copies.append(
            pltpu.make_async_remote_copy(
                src_ref=tile_ref,
                dst_ref=out_ref.at[slot],
                send_sem=send_sem.at[n],
                recv_sem=recv_sem.at[n],
                device_id=device(dy, dx),
                device_id_type=MESH,
            )
        )
        copies[-1].start()
    own.wait()
    for copy in copies:
        copy.wait()


def exchange(tile):
    return pl.pallas_call(
        exchange_kernel,
        out_shape=jax.ShapeDtypeStruct((9,) + tile.shape, tile.dtype),
        in_specs=[pl.BlockSpec(memory_space=pltpu.VMEM)],
        out_specs=pl.BlockSpec(memory_space=pltpu.VMEM),
        scratch_shapes=[
            pltpu.SemaphoreType.DMA((8,)),
            pltpu.SemaphoreType.DMA((8,)),
            pltpu.SemaphoreType.DMA,
        ],
        compiler_params=pltpu.CompilerParams(collective_id=0, has_side_effects=True),
        name="exchange_tiles",
    )(tile)


def store_shifted(ref, pair, parity, start, count, value, row):
    below = jnp.where(row == 0, 0.0, pltpu.roll(value, 1, axis=1))
    above = jnp.where(row == Z - 1, 0.0, pltpu.roll(value, Z - 1, axis=1))
    for shift, part in enumerate((below, value, above)):
        ref[shift, pair, parity, pl.ds(start, count)] = part.astype(BF)


def conv_operand(ref, pair, start, count):
    parts = []
    for shift in range(3):
        for offset in range(4):
            for k in range(2):
                part = ref[shift, pair + k, offset % 2, pl.ds(start + offset // 2, count)]
                parts.append(part.reshape(count * Z, 2 * C))
    return jnp.concatenate(parts, axis=1)


def build_conv_weights(kernel_ref, out_ref):
    zero = jnp.zeros((C, C), BF)
    for shift in range(3):
        for offset in range(4):
            for source in range(4):
                rows = ((shift * 4 + offset) * 4 + source) * C
                for qx in range(2):
                    blocks = []
                    for qy in range(2):
                        dx, dy = offset - qx, source - qy
                        inside = 0 <= dx < 3 and 0 <= dy < 3
                        blocks.append(kernel_ref[(shift * 3 + dy) * 3 + dx] if inside else zero)
                    out_ref[rows : rows + C, qx * 128 : qx * 128 + 128] = jnp.concatenate(blocks, axis=1)


def zero_pairs(ref, pair, lower=None):
    count = ref.shape[3]
    lane = lax.broadcasted_iota(jnp.int32, (Z, 2 * C), 1)

    def body(i, carry):
        for shift in range(3):
            for parity in range(2):
                if lower is None:
                    ref[shift, pair, parity, i] = jnp.zeros((Z, 2 * C), BF)
                else:
                    old = ref[shift, pair, parity, i].astype(F32)
                    keep = lane >= C if lower else lane < C
                    ref[shift, pair, parity, i] = jnp.where(keep, old, 0.0).astype(BF)
        return carry

    lax.fori_loop(0, count, body, 0)


def zero_columns(ref, columns):
    for pair in range(ref.shape[1]):
        for x in columns:
            for shift in range(3):
                ref[shift, pair, x % 2, x // 2] = jnp.zeros((Z, 2 * C), BF)


def coverage_of(position, length):
    total = jnp.zeros(position.shape, F32)
    for b in range(2 * R + 1):
        source = position - (b - R)
        total += jnp.where((source >= 0) & (source < length), float(R + 1 - abs(b - R)), 0.0)
    return total


def compute_kernel(
    tiles_ref, place_ref, first_ref, second_ref, third_ref, head_ref, columns_ref, blend_ref,
    out_ref,
    w1, w2, w3, wh, main, edge, qf, qb, stem, inner, pred, total,
):
    gx, gy = lax.axis_index("gx"), lax.axis_index("gy")
    nx, ny = lax.axis_size("gx"), lax.axis_size("gy")
    at_low_x, at_high_x = gx == 0, gx == nx - 1
    at_low_y, at_high_y = gy == 0, gy == ny - 1

    build_conv_weights(second_ref, w2)
    build_conv_weights(third_ref, w3)
    for pair in range(STEM_PAIRS):
        w1[pair] = jnp.dot(place_ref[pair], first_ref[...], preferred_element_type=F32).astype(BF)
    for py in range(2):
        wh[py * C : py * C + C, :] = jnp.dot(
            head_ref[...], columns_ref[py], preferred_element_type=F32
        ).astype(BF)

    lane8 = lax.broadcasted_iota(jnp.int32, (TY, TX), 1)
    for buffer in (main, edge):
        buffer[0] = jnp.zeros((3 * TY, TX), F32)
        buffer[Z + 1] = jnp.zeros((3 * TY, TX), F32)
    right_ok = jnp.where(at_high_x, 0, 64)
    left_ok = jnp.where(at_low_x, 128, 64)

    def spread_z(z, carry):
        for ty in range(3):
            middle = tiles_ref[ty * 3 + 1, z].astype(F32)
            left = tiles_ref[ty * 3, z].astype(F32)
            right = tiles_ref[ty * 3 + 2, z].astype(F32)
            sides = jnp.where(lane8 < right_ok, right, jnp.where(lane8 >= left_ok, left, 0.0))
            if ty == 0:
                middle, sides = jnp.where(at_low_y, 0.0, middle), jnp.where(at_low_y, 0.0, sides)
            if ty == 2:
                middle, sides = jnp.where(at_high_y, 0.0, middle), jnp.where(at_high_y, 0.0, sides)
            main[z + 1, ty * TY : ty * TY + TY, :] = middle
            edge[z + 1, ty * TY : ty * TY + TY, :] = sides
        return carry

    lax.fori_loop(0, Z, spread_z, 0)
    filler = jnp.zeros((128 - 9 * TY, TX), F32)
    for z in range(Z):
        middle = jnp.concatenate([main[z], main[z + 1], main[z + 2], filler], axis=0).T
        sides = jnp.concatenate([edge[z], edge[z + 1], edge[z + 2], filler], axis=0).T
        qf[pl.ds(8 * Z + z, TX, stride=Z), :] = middle
        qf[pl.ds(z, 8, stride=Z), :] = sides[120:128]
        qf[pl.ds(136 * Z + z, 8, stride=Z), :] = sides[0:8]

    def round_pair(m, carry):
        for parity in range(2):
            qb[parity, m] = qf[pl.ds(pl.multiple_of((2 * m + parity) * Z, Z), Z), :].astype(BF)
        return carry

    lax.fori_loop(0, 72, round_pair, 0)

    row = lax.broadcasted_iota(jnp.int32, (XT, Z, 2 * C), 1)

    def stem_body(step, carry):
        pair, j = step // 4, (step % 4) * XT
        parts = []
        for offset in range(4):
            at = offset + 3
            parts.append(qb[at % 2, pl.ds(j + at // 2, XT)].reshape(XT * Z, 128))
        acc = jnp.dot(jnp.concatenate(parts, axis=1), w1[pair], preferred_element_type=F32)
        acc = jnp.maximum(acc, 0.0)
        for qx in range(2):
            value = acc[:, qx * 128 : qx * 128 + 128].reshape(XT, Z, 128)
            store_shifted(stem, pair, qx, j, XT, value, row)
        return carry

    lax.fori_loop(0, STEM_PAIRS * 4, stem_body, 0)

    @pl.when(at_low_y)
    def _():
        zero_pairs(stem, 0)
        zero_pairs(stem, 1)

    @pl.when(at_high_y)
    def _():
        zero_pairs(stem, 6)
        zero_pairs(stem, 7)

    @pl.when(at_low_x)
    def _():
        zero_columns(stem, range(4))

    @pl.when(at_high_x)
    def _():
        zero_columns(stem, range(132, 136))

    for pair in range(STEM_PAIRS):
        for shift in range(3):
            for parity in range(2):
                stem[shift, pair, parity, STEM_X] = jnp.zeros((Z, 2 * C), BF)

    def inner_body(step, carry):
        pair, j = step // 4, (step % 4) * XT
        acc = jnp.dot(conv_operand(stem, pair, j, XT), w2[...], preferred_element_type=F32)
        acc = jnp.maximum(acc, 0.0)
        for qx in range(2):
            value = acc[:, qx * 128 : qx * 128 + 128].reshape(XT, Z, 128)
            store_shifted(inner, pair, qx, j, XT, value, row)
        return carry

    lax.fori_loop(0, INNER_PAIRS * 4, inner_body, 0)

    @pl.when(at_low_y)
    def _():
        zero_pairs(inner, 0)
        zero_pairs(inner, 1, lower=True)

    @pl.when(at_high_y)
    def _():
        zero_pairs(inner, 5, lower=False)
        zero_pairs(inner, 6)

    @pl.when(at_low_x)
    def _():
        zero_columns(inner, range(3))

    @pl.when(at_high_x)
    def _():
        zero_columns(inner, range(131, 134))

    for pair in range(INNER_PAIRS):
        for shift in range(3):
            for parity in range(2):
                inner[shift, pair, parity, STEM_X] = jnp.zeros((Z, 2 * C), BF)

    def block_body(step, carry):
        pair, j = step // 4, (step % 4) * XT
        acc = jnp.dot(conv_operand(inner, pair, j, XT), w3[...], preferred_element_type=F32)
        for qx in range(2):
            old = stem[1, pair + 1, qx, pl.ds(j + 1, XT)].reshape(XT * Z, 128).astype(F32)
            value = jnp.maximum(acc[:, qx * 128 : qx * 128 + 128] + old, 0.0).astype(BF)
            logits = jnp.dot(value, wh[...], preferred_element_type=F32)
            pred[pair, qx, pl.ds(j, XT)] = jnp.tanh(logits).astype(BF).reshape(XT, Z, 256)
        return carry

    lax.fori_loop(0, BLOCK_PAIRS * 4, block_body, 0)

    def zero_pred(pair):
        def body(i, carry):
            for parity in range(2):
                pred[pair, parity, i] = jnp.zeros((Z, 256), BF)
            return carry

        lax.fori_loop(0, BLOCK_X, body, 0)

    @pl.when(at_low_y)
    def _():
        zero_pred(0)

    @pl.when(at_high_y)
    def _():
        zero_pred(5)

    @pl.when(at_low_x)
    def _():
        for pair in range(BLOCK_PAIRS):
            for parity in range(2):
                pred[pair, parity, 0] = jnp.zeros((Z, 256), BF)

    @pl.when(at_high_x)
    def _():
        for pair in range(BLOCK_PAIRS):
            for parity in range(2):
                pred[pair, parity, 65] = jnp.zeros((Z, 256), BF)

    lanes = lax.broadcasted_iota(jnp.int32, (1, Z, 128), 2)
    XB = 8

    def blend_body(step, carry):
        j = step * XB
        for qx in range(2):
            operands = []
            for target in range(TY // 2):
                for half in range(2):
                    chosen = None
                    for a in (0, 1, 2) if half == 0 else (2, 3, 4):
                        at = qx - a + 4
                        for k in range(3):
                            part = pred[target + k, at % 2, pl.ds(j + at // 2, XB), :, half * 128 : half * 128 + 128]
                            if chosen is None:
                                chosen = part
                            else:
                                group = (a - (0 if half == 0 else 2)) * 3 + k
                                chosen = jnp.where(lanes >= GROUP_START[half][group], part, chosen)
                    operands.append(chosen.reshape(XB * Z, 128))
            added = jnp.dot(jnp.concatenate(operands, axis=1), blend_ref[...], preferred_element_type=F32)
            total[qx, pl.ds(pl.multiple_of(j * Z, XB * Z), XB * Z), :] = added
        return carry

    lax.fori_loop(0, TX // 2 // XB, blend_body, 0)

    y = gy * TY + lax.broadcasted_iota(jnp.int32, (TY, TX), 0)
    x = gx * TX + lane8
    scale = 0.5 / (coverage_of(y, ny * TY) * coverage_of(x, nx * TX))

    for z in range(Z):
        even = total[0, pl.ds(z, TX // 2, stride=Z), :]
        odd = total[1, pl.ds(z, TX // 2, stride=Z), :]
        both = jnp.stack([even, odd], axis=1).reshape(TX, 128).T
        for c in range(3):
            out_ref[c, z] = 0.5 + both[c * TY : c * TY + TY, :] * scale


def lane_plan():
    plan, starts = [], []
    for half in range(2):
        lanes, begin = [], []
        for a in (0, 1, 2) if half == 0 else (2, 3, 4):
            for k in range(3):
                begin.append(len(lanes))
                for py in range(2):
                    if a == 2 and py != half:
                        continue
                    for b in range(5):
                        if -((py + b - 4) // 2) == k:
                            lanes += [(a, py, b, c) for c in range(3)]
        plan.append(lanes)
        starts.append(begin)
    return plan, starts


LANES, GROUP_START = lane_plan()


def constants():
    place = np.zeros((STEM_PAIRS, 4, 128, 128), np.float32)
    for pair in range(STEM_PAIRS):
        for qx in range(2):
            for qy in range(2):
                for dz in range(3):
                    for dy in range(3):
                        for dx in range(3):
                            y = 3 + 2 * pair + qy + dy
                            place[pair, qx + dx, dz * 24 + y, (qx * 2 + qy) * 32 + (dz * 3 + dy) * 3 + dx] = 1
    columns = np.zeros((2, 75, 256), np.float32)
    blend = np.zeros((TY // 2, 256, 128), np.float32)
    for half in range(2):
        for n, (a, py, b, c) in enumerate(LANES[half]):
            columns[py, (a * 5 + b) * 3 + c, half * 128 + n] = 0.5
            for target in range(TY // 2):
                weight = (R + 1 - abs(a - R)) * (R + 1 - abs(b - R))
                blend[target, half * 128 + n, c * TY + 2 * target + (py + b) % 2] = weight
    return (
        jnp.asarray(place.reshape(STEM_PAIRS, 512, 128), BF),
        jnp.asarray(columns, BF),
        jnp.asarray(blend.reshape(-1, 128), BF),
    )


def local(intensity, first_kernel, second_kernel, third_kernel, head_weight):
    tiles = exchange(intensity)
    place, columns, blend = constants()
    taps = jnp.pad(first_kernel.reshape(27, C), ((0, 5), (0, 0)))
    first = (jnp.eye(4, dtype=BF)[:, None, :, None] * taps[None, :, None, :]).reshape(128, 256)
    padded = STEM_X + 2
    return pl.pallas_call(
        compute_kernel,
        out_shape=jax.ShapeDtypeStruct((3, Z, TY, TX), F32),
        in_specs=[pl.BlockSpec(memory_space=pltpu.VMEM)] * 8,
        out_specs=pl.BlockSpec(memory_space=pltpu.VMEM),
        scratch_shapes=[
            pltpu.VMEM((STEM_PAIRS, 512, 256), BF),
            pltpu.VMEM((3072, 256), BF),
            pltpu.VMEM((3072, 256), BF),
            pltpu.VMEM((128, 256), BF),
            pltpu.VMEM((Z + 2, 3 * TY, TX), F32),
            pltpu.VMEM((Z + 2, 3 * TY, TX), F32),
            pltpu.VMEM((144 * Z, 128), F32),
            pltpu.VMEM((2, 72, Z, 128), BF),
            pltpu.VMEM((3, STEM_PAIRS, 2, padded, Z, 128), BF),
            pltpu.VMEM((3, INNER_PAIRS, 2, padded, Z, 128), BF),
            pltpu.VMEM((BLOCK_PAIRS, 2, STEM_X, Z, 256), BF),
            pltpu.VMEM((2, TX // 2 * Z, 128), F32),
        ],
        compiler_params=pltpu.CompilerParams(vmem_limit_bytes=60 * 2**20),
        name="convnet",
    )(
        tiles, place, first,
        second_kernel.reshape(27, C, C), third_kernel.reshape(27, C, C), head_weight, columns, blend,
    )


def solution(mesh):
    in_specs = (P(None, "gy", "gx"), P(), P(), P(), P())
    out_specs = P(None, None, "gy", "gx")
    return jax.shard_map(local, mesh=mesh, in_specs=in_specs, out_specs=out_specs, check_vma=False)
```

time: 605 us -> 76.7 us (0.13)
  the two profiles are of different devices: /device:TPU:1 before, /device:TPU:0 now
where the time goes in v1:
time: 76.7 us; the launch traced here: 76.5 us
  Pallas kernels  74.8 us (98%)
  local copies, waits for them, and re-layouts  1.5 us (2%)
    pallas_call x1, Pallas kernels, local(): pl.pallas_call(compute_kernel, out_shape=jax.ShapeDtypeStruct((3, Z, TY,...  58 us
    pallas_call x1, Pallas kernels, exchange(): pl.pallas_call(exchange_kernel, out_shape=jax.ShapeDtypeStruct((9,) + til...  16.8 us

profile of v1, /device:TPU:0, one launch (start us, length us, event | category | flops | bytes accessed | tf_op | source)
XLA Modules:
  0.0 76.5 jit_solution(15470319652840069898)
XLA Ops:
  0.0 0.7 reshape.22
  0.7 0.1 broadcast_multiply_fusion
  0.9 0.8 %mul.20.first_ref = bf16[128,256]{1,0:T(8,128)(2,1)} reshape(bf16[4,32,4,64]{3,2,1,0:T(4,128)(2,1)S(1)} %broadcast_multiply_fusion) | data formatting | bytes 131072 | tf_op jit(solution)/shard_map/mul | solution.py:401
  1.6 16.8 %exchange_tiles.1.tiles_ref = bf16[9,16,8,128]{3,2,1,0:T(8,128)(2,1)} custom-call(bf16[16,8,128]{2,1,0:T(8,128)(2,1)} %tile_ref.1), custom_call_target="tpu_custom_call" | custom-call | tf_op jit(solution)/shard_map/exchange_tiles/pallas_call | solution.py:63
  18.4 58.0 %convnet.1 = f32[3,16,8,128]{3,2,1,0:T(8,128)} custom-call(bf16[9,16,8,128]{3,2,1,0:T(8,128)(2,1)} %exchange_tiles.1.tiles_ref, bf16[8,512,128]{2,1,0:T(8,128)(2,1)} %constant.9.clone.place_ref, bf16[128,256]{1,0:T(8,128)(2,1)} %mul.20.first_ref, bf16[27,64,64]{2,1,0:T(8,128)(2,1)} %bitcast.4, bf16[27,64,64]{2,1,0:T(8,128)(2,1)} %bitcast.5, ...), custom_call_target="tpu_custom_call" | custom-call | tf_op jit(solution)/shard_map/convnet/pallas_call | solution.py:403
  (2 shorter events, 0.0 us)

commit v2 on v1

v2 whole, which is shorter than its diff:
```python
import functools

import jax
import jax.numpy as jnp
import numpy as np
from jax import lax
from jax.experimental import pallas as pl
from jax.experimental.pallas import tpu as pltpu
from jax.sharding import PartitionSpec as P

R = 2
C = 64
Z = 16
TY = 8
TX = 128
BF = jnp.bfloat16
F32 = jnp.float32
MESH = pl.DeviceIdType.MESH


STEM_PAIRS = 6
INNER_PAIRS = 5
BLOCK_PAIRS = 4
STEM_X = 68
INNER_X = 67
BLOCK_X = 66
XB = 16
AROUND = [(dy, dx) for dy in (-1, 0, 1) for dx in (-1, 0, 1) if (dy, dx) != (0, 0)]


def store_shifted(ref, pair, parity, value):
    count = value.shape[0]
    row = lax.broadcasted_iota(jnp.int32, (1, Z, 2 * C), 1)
    below = jnp.where(row == 0, 0.0, pltpu.roll(value, 1, axis=1))
    above = jnp.where(row == Z - 1, 0.0, pltpu.roll(value, Z - 1, axis=1))
    for shift, part in enumerate((below, value, above)):
        ref[shift, pair, parity, 0:count] = part.astype(BF)


def conv_operand(ref, pair, count):
    parts = []
    for shift in range(3):
        for offset in range(4):
            for k in range(2):
                first = offset // 2
                part = ref[shift, pair + k, offset % 2, first : first + count]
                parts.append(part.reshape(count * Z, 2 * C))
    return jnp.concatenate(parts, axis=1)


def build_conv_weights(kernel_ref, out_ref):
    zero = jnp.zeros((C, C), BF)
    for shift in range(3):
        for offset in range(4):
            for source in range(4):
                rows = ((shift * 4 + offset) * 4 + source) * C
                for qx in range(2):
                    blocks = []
                    for qy in range(2):
                        dx, dy = offset - qx, source - qy
                        inside = 0 <= dx < 3 and 0 <= dy < 3
                        blocks.append(kernel_ref[(shift * 3 + dy) * 3 + dx] if inside else zero)
                    out_ref[rows : rows + C, qx * 128 : qx * 128 + 128] = jnp.concatenate(blocks, axis=1)


def zero_columns(ref, columns):
    for pair in range(ref.shape[1]):
        for x in columns:
            for shift in range(3):
                ref[shift, pair, x % 2, x // 2] = jnp.zeros((Z, 2 * C), BF)


def coverage_of(position, length):
    total = jnp.zeros(position.shape, F32)
    for b in range(2 * R + 1):
        source = position - (b - R)
        total += jnp.where((source >= 0) & (source < length), float(R + 1 - abs(b - R)), 0.0)
    return total


def compute_kernel(
    tile_ref, place_hbm, first_ref, second_hbm, third_hbm, head_ref, columns_ref, blend_hbm,
    out_ref,
    place, second, third, blend,
    strips, rows_in, sides_in, edge_out, edge_in,
    taps, w1, w2, w3, wh, main, edge, qf, qb, stem, inner, pred, total,
    load_sem, send_sem, recv_sem, edge_send_sem, edge_recv_sem,
):
    gx, gy = lax.axis_index("gx"), lax.axis_index("gy")
    nx, ny = lax.axis_size("gx"), lax.axis_size("gy")
    at_low_x, at_high_x = gx == 0, gx == nx - 1
    at_low_y, at_high_y = gy == 0, gy == ny - 1

    def device(dy, dx):
        return (lax.rem(gx + dx + nx, nx), lax.rem(gy + dy + ny, ny))

    barrier = pltpu.get_barrier_semaphore()
    for dy, dx in AROUND:
        pl.semaphore_signal(barrier, inc=1, device_id=device(dy, dx), device_id_type=MESH)
    loads = []
    for n, (source, target) in enumerate(
        ((second_hbm, second), (third_hbm, third), (place_hbm, place), (blend_hbm, blend))
    ):
        loads.append(pltpu.make_async_copy(source, target, load_sem.at[n]))
        loads[-1].start()

    turned = tile_ref[...].astype(F32).reshape(Z * TY, TX).T
    strips[0] = turned[0:16].astype(BF)
    strips[1] = turned[TX - 16 : TX].astype(BF)
    pl.semaphore_wait(barrier, len(AROUND))
    copies = []
    for n, (dy, dx) in enumerate(AROUND):
        if dx == 0:
            source, target = tile_ref, rows_in.at[0 if dy == 1 else 1]
        else:
            source, target = strips.at[0 if dx == -1 else 1], sides_in.at[1 - dy, 0 if dx == 1 else 1]
        copies.append(
            pltpu.make_async_remote_copy(
                src_ref=source,
                dst_ref=target,
                send_sem=send_sem.at[n],
                recv_sem=recv_sem.at[n],
                device_id=device(dy, dx),
                device_id_type=MESH,
            )
        )
        copies[-1].start()

    for load in loads:
        load.wait()
    build_conv_weights(second, w2)
    build_conv_weights(third, w3)
    taps[...] = jnp.zeros((32, C), F32)
    for n in range(9):
        taps[3 * n : 3 * n + 3, :] = first_ref[n].astype(F32)
    tap = taps[...].astype(BF)
    nothing = jnp.zeros((32, C), BF)
    spread = jnp.concatenate(
        [jnp.concatenate([tap if i == q else nothing for i in range(4)], axis=1) for q in range(4)], axis=0
    )
    for pair in range(STEM_PAIRS):
        w1[pair] = jnp.dot(place[pair], spread, preferred_element_type=F32).astype(BF)
    for py in range(2):
        wh[py * C : py * C + C, :] = jnp.dot(
            head_ref[...], columns_ref[py], preferred_element_type=F32
        ).astype(BF)

    for copy in copies:
        copy.wait()

    lane8 = lax.broadcasted_iota(jnp.int32, (TY, TX), 1)
    lane128 = lax.broadcasted_iota(jnp.int32, (Z * TY, TX), 1)
    for buffer in (main, edge):
        buffer[0] = jnp.zeros((3 * TY, TX), F32)
        buffer[Z + 1] = jnp.zeros((3 * TY, TX), F32)
    right_ok = jnp.where(at_high_x, 0, 64)
    left_ok = jnp.where(at_low_x, 128, 64)
    between = jnp.zeros((TX - 32, Z * TY), F32)
    for ty in range(3):
        left, right = sides_in[ty, 0].astype(F32), sides_in[ty, 1].astype(F32)
        sides = jnp.concatenate([right, between, left], axis=0).T
        sides = jnp.where((lane128 < right_ok) | (lane128 >= left_ok), sides, 0.0)
        middle = (tile_ref[...] if ty == 1 else rows_in[ty // 2]).astype(F32)
        sides = sides.reshape(Z, TY, TX)
        if ty != 1:
            outside = at_low_y if ty == 0 else at_high_y
            middle, sides = jnp.where(outside, 0.0, middle), jnp.where(outside, 0.0, sides)
        main[1 : Z + 1, ty * TY : ty * TY + TY, :] = middle
        edge[1 : Z + 1, ty * TY : ty * TY + TY, :] = sides
    filler = jnp.zeros((128 - 9 * TY, TX), F32)
    for z in range(Z):
        middle = jnp.concatenate([main[z], main[z + 1], main[z + 2], filler], axis=0).T
        sides = jnp.concatenate([edge[z], edge[z + 1], edge[z + 2], filler], axis=0).T
        qf[pl.ds(8 * Z + z, TX, stride=Z), :] = middle
        qf[pl.ds(z, 8, stride=Z), :] = sides[120:128]
        qf[pl.ds(136 * Z + z, 8, stride=Z), :] = sides[0:8]

    def round_pair(m, carry):
        for parity in range(2):
            qb[parity, m] = qf[pl.ds(pl.multiple_of((2 * m + parity) * Z, Z), Z), :].astype(BF)
        return carry

    lax.fori_loop(0, 72, round_pair, 0, unroll=4)

    def stem_body(pair, carry):
        parts = []
        for offset in range(4):
            at = offset + 3
            parts.append(qb[at % 2, at // 2 : at // 2 + STEM_X].reshape(STEM_X * Z, 128))
        acc = jnp.dot(jnp.concatenate(parts, axis=1), w1[pair], preferred_element_type=F32)
        outside = (at_low_y & (pair == 0)) | (at_high_y & (pair == STEM_PAIRS - 1))
        acc = jnp.maximum(acc, 0.0) * jnp.where(outside, 0.0, 1.0)
        for qx in range(2):
            value = acc[:, qx * 128 : qx * 128 + 128].reshape(STEM_X, Z, 128)
            store_shifted(stem, pair, qx, value)
        return carry

    lax.fori_loop(0, STEM_PAIRS, stem_body, 0)

    @pl.when(at_low_x)
    def _():
        zero_columns(stem, range(4))

    @pl.when(at_high_x)
    def _():
        zero_columns(stem, range(132, 136))

    upper = (lax.broadcasted_iota(jnp.int32, (1, 128), 1) // C).astype(jnp.int32)

    def inner_body(pair, carry):
        acc = jnp.dot(conv_operand(stem, pair, INNER_X), w2[...], preferred_element_type=F32)
        low = jnp.where(at_low_y & (pair == 0), 0, -1)
        high = jnp.where(at_high_y & (pair == INNER_PAIRS - 1), 1, -1)
        keep = jnp.where((upper == low) | (upper == high), 0.0, 1.0)
        for qx in range(2):
            value = jnp.maximum(acc[:, qx * 128 : qx * 128 + 128], 0.0) * keep
            store_shifted(inner, pair, qx, value.reshape(INNER_X, Z, 128))
        return carry

    lax.fori_loop(0, INNER_PAIRS, inner_body, 0)

    @pl.when(at_low_x)
    def _():
        zero_columns(inner, range(3))

    @pl.when(at_high_x)
    def _():
        zero_columns(inner, range(131, 134))

    def block_body(pair):
        acc = jnp.dot(conv_operand(inner, pair, BLOCK_X), w3[...], preferred_element_type=F32)
        for qx in range(2):
            old = stem[1, pair + 1, qx, 1 : 1 + BLOCK_X].reshape(BLOCK_X * Z, 128).astype(F32)
            value = jnp.maximum(acc[:, qx * 128 : qx * 128 + 128] + old, 0.0).astype(BF)
            logits = jnp.dot(value, wh[...], preferred_element_type=F32)
            pred[pair, qx] = jnp.tanh(logits).astype(BF).reshape(BLOCK_X, Z, 256)

        @pl.when(at_low_x)
        def _():
            for parity in range(2):
                pred[pair, parity, 0] = jnp.zeros((Z, 256), BF)

        @pl.when(at_high_x)
        def _():
            for parity in range(2):
                pred[pair, parity, BLOCK_X - 1] = jnp.zeros((Z, 256), BF)

    lanes = lax.broadcasted_iota(jnp.int32, (1, Z, 128), 2)

    def blend_rows(targets, first):
        def body(step, carry):
            j = step * XB
            for qx in range(2):
                operands = []
                for target in targets:
                    for half in range(2):
                        chosen = None
                        for n, a in enumerate((0, 1, 2) if half == 0 else (2, 3, 4)):
                            at = qx - a + 4
                            for k in range(3):
                                pair = target + k - 1
                                if not 0 <= pair < BLOCK_PAIRS:
                                    continue
                                part = pred[pair, at % 2, pl.ds(j + at // 2, XB), :, half * 128 : half * 128 + 128]
                                if chosen is None:
                                    chosen = part
                                else:
                                    chosen = jnp.where(lanes >= GROUP_START[half][n * 3 + k], part, chosen)
                        operands.append(chosen.reshape(XB * Z, 128))
                added = jnp.dot(
                    jnp.concatenate(operands, axis=1),
                    blend[first : first + 256 * len(targets), :],
                    preferred_element_type=F32,
                )
                total[qx, pl.ds(pl.multiple_of(j * Z, XB * Z), XB * Z), :] = added
            return carry

        lax.fori_loop(0, TX // 2 // XB, body, 0)

    def turned_total(z):
        even = total[0, pl.ds(z, TX // 2, stride=Z), :]
        odd = total[1, pl.ds(z, TX // 2, stride=Z), :]
        return jnp.stack([even, odd], axis=1).reshape(TX, 128).T

    def outer_body(step, carry):
        block_body(step * (BLOCK_PAIRS - 1))
        return carry

    lax.fori_loop(0, 2, outer_body, 0)
    blend_rows((-1, BLOCK_PAIRS), 0)
    for z in range(Z):
        both = turned_total(z)
        for side in range(2):
            edge_out[side, z] = both[24 + 8 * side : 32 + 8 * side]
    edges = []
    for side, dy in enumerate((-1, 1)):
        edges.append(
            pltpu.make_async_remote_copy(
                src_ref=edge_out.at[side],
                dst_ref=edge_in.at[side],
                send_sem=edge_send_sem.at[side],
                recv_sem=edge_recv_sem.at[side],
                device_id=device(dy, 0),
                device_id_type=MESH,
            )
        )
        edges[-1].start()

    def middle_body(step, carry):
        block_body(step + 1)
        return carry

    lax.fori_loop(0, BLOCK_PAIRS - 2, middle_body, 0)
    blend_rows(tuple(range(BLOCK_PAIRS)), 512)

    y8 = lax.broadcasted_iota(jnp.int32, (TY, TX), 0)
    scale = 0.5 / (coverage_of(gy * TY + y8, ny * TY) * coverage_of(gx * TX + lane8, nx * TX))
    from_above = (y8 < 2) & (gy > 0)
    from_below = (y8 >= TY - 2) & (gy < ny - 1)
    for copy in edges:
        copy.wait()
    for z in range(Z):
        both = turned_total(z)
        below, above = edge_in[0, z], edge_in[1, z]
        for c in range(3):
            added = both[c * TY : c * TY + TY, :]
            added += jnp.where(from_above, above if c == 0 else pltpu.roll(above, TY - 2 * c, axis=0), 0.0)
            added += jnp.where(from_below, pltpu.roll(below, TY - 2 - 2 * c, axis=0), 0.0)
            out_ref[c, z] = 0.5 + added * scale


def lane_plan():
    plan, starts = [], []
    for half in range(2):
        lanes, begin = [], []
        for a in (0, 1, 2) if half == 0 else (2, 3, 4):
            for k in range(3):
                begin.append(len(lanes))
                for py in range(2):
                    if a == 2 and py != half:
                        continue
                    for b in range(5):
                        if -((py + b - 4) // 2) == k:
                            lanes += [(a, py, b, c) for c in range(3)]
        plan.append(lanes)
        starts.append(begin)
    return plan, starts


LANES, GROUP_START = lane_plan()


def constants():
    place = np.zeros((STEM_PAIRS, 4, 128, 128), np.float32)
    for pair in range(STEM_PAIRS):
        for qx in range(2):
            for qy in range(2):
                for dz in range(3):
                    for dy in range(3):
                        for dx in range(3):
                            y = 5 + 2 * pair + qy + dy
                            place[pair, qx + dx, dz * 24 + y, (qx * 2 + qy) * 32 + (dz * 3 + dy) * 3 + dx] = 1
    columns = np.zeros((2, 75, 256), np.float32)
    targets = (-1, BLOCK_PAIRS) + tuple(range(BLOCK_PAIRS))
    blend = np.zeros((len(targets), 256, 128), np.float32)
    for half in range(2):
        for n, (a, py, b, c) in enumerate(LANES[half]):
            columns[py, (a * 5 + b) * 3 + c, half * 128 + n] = 0.5
            weight = (R + 1 - abs(a - R)) * (R + 1 - abs(b - R))
            for i, target in enumerate(targets):
                if not 0 <= target + 1 - (py + b) // 2 < BLOCK_PAIRS:
                    continue
                qy = (py + b) % 2
                if target < 0:
                    lane = 24 + 2 * c + qy
                elif target == BLOCK_PAIRS:
                    lane = 32 + 2 * c + qy
                else:
                    lane = c * TY + 2 * target + qy
                blend[i, half * 128 + n, lane] = weight
    return (
        jnp.asarray(place.reshape(STEM_PAIRS, 512, 128), BF),
        jnp.asarray(columns, BF),
        jnp.asarray(blend.reshape(-1, 128), BF),
    )


def local(intensity, first_kernel, second_kernel, third_kernel, head_weight):
    place, columns, blend = constants()
    vmem = pl.BlockSpec(memory_space=pltpu.VMEM)
    hbm = pl.BlockSpec(memory_space=pl.ANY)
    return pl.pallas_call(
        compute_kernel,
        out_shape=jax.ShapeDtypeStruct((3, Z, TY, TX), F32),
        in_specs=[vmem, hbm, vmem, hbm, hbm, vmem, vmem, hbm],
        out_specs=vmem,
        scratch_shapes=[
            pltpu.VMEM(place.shape, BF),
            pltpu.VMEM((27, C, C), BF),
            pltpu.VMEM((27, C, C), BF),
            pltpu.VMEM(blend.shape, BF),
            pltpu.VMEM((2, 16, Z * TY), BF),
            pltpu.VMEM((2, Z, TY, TX), BF),
            pltpu.VMEM((3, 2, 16, Z * TY), BF),
            pltpu.VMEM((2, Z, TY, TX), F32),
            pltpu.VMEM((2, Z, TY, TX), F32),
            pltpu.VMEM((32, C), F32),
            pltpu.VMEM((STEM_PAIRS, 512, 256), BF),
            pltpu.VMEM((3072, 256), BF),
            pltpu.VMEM((3072, 256), BF),
            pltpu.VMEM((128, 256), BF),
            pltpu.VMEM((Z + 2, 3 * TY, TX), F32),
            pltpu.VMEM((Z + 2, 3 * TY, TX), F32),
            pltpu.VMEM((144 * Z, 128), F32),
            pltpu.VMEM((2, 72, Z, 128), BF),
            pltpu.VMEM((3, STEM_PAIRS, 2, STEM_X, Z, 128), BF),
            pltpu.VMEM((3, INNER_PAIRS, 2, INNER_X, Z, 128), BF),
            pltpu.VMEM((BLOCK_PAIRS, 2, BLOCK_X, Z, 256), BF),
            pltpu.VMEM((2, TX // 2 * Z, 128), F32),
            pltpu.SemaphoreType.DMA((4,)),
            pltpu.SemaphoreType.DMA((8,)),
            pltpu.SemaphoreType.DMA((8,)),
            pltpu.SemaphoreType.DMA((2,)),
            pltpu.SemaphoreType.DMA((2,)),
        ],
        compiler_params=pltpu.CompilerParams(
            collective_id=0, has_side_effects=True, vmem_limit_bytes=56 * 2**20
        ),
        name="convnet",
    )(
        intensity, place, first_kernel.reshape(9, 3, C),
        second_kernel.reshape(27, C, C), third_kernel.reshape(27, C, C), head_weight, columns, blend,
    )


def solution(mesh):
    in_specs = (P(None, "gy", "gx"), P(), P(), P(), P())
    out_specs = P(None, None, "gy", "gx")
    return jax.shard_map(local, mesh=mesh, in_specs=in_specs, out_specs=out_specs, check_vma=False)
```

time: 76.7 us -> 46.3 us (0.60)
  the two profiles are of different devices: /device:TPU:0 before, /device:TPU:1 now
where the time goes in v2:
time: 46.3 us; the launch traced here: 46.1 us
  Pallas kernels  44.5 us (96%)
  local copies, waits for them, and re-layouts  1.62 us (3%)
    pallas_call x1, Pallas kernels, local(): pl.pallas_call(compute_kernel, out_shape=jax.ShapeDtypeStruct((3, Z, TY,...  44.5 us
    unnamed x1, local copies, waits for them, and re-layouts  1.62 us

profile of v2, /device:TPU:1, one launch (start us, length us, event | category | flops | bytes accessed | tf_op | source)
XLA Modules:
  0.0 46.1 jit_solution(4371772292083557670)
XLA Ops:
  0.0 44.5 %convnet.1 = f32[3,16,8,128]{3,2,1,0:T(8,128)} custom-call(bf16[16,8,128]{2,1,0:T(8,128)(2,1)} %tile_ref.1, bf16[6,512,128]{2,1,0:T(8,128)(2,1)} %constant.6.clone.place_hbm, bf16[9,3,64]{2,1,0:T(4,128)(2,1)} %bitcast.5, bf16[27,64,64]{2,1,0:T(8,128)(2,1)} %bitcast.3, bf16[27,64,64]{2,1,0:T(8,128)(2,1)} %bitcast.4, bf16[64,75]{1,0:T(8,128)(2,1)} %head_ref.1, ...), custom_call_target="tpu_custom_call" | custom-call | tf_op jit(solution)/shard_map/convnet/pallas_call | solution.py:392
  44.5 1.6 %copy.10 = f32[3,16,8,128]{3,2,1,0:T(8,128)} copy(f32[3,16,8,128]{3,2,1,0:T(8,128)} %convnet.1) | data formatting | bytes 393216

commit v3 on v2

v3 whole, which is shorter than its diff:
```python
import functools

import jax
import jax.numpy as jnp
import numpy as np
from jax import lax
from jax.experimental import pallas as pl
from jax.experimental.pallas import tpu as pltpu
from jax.sharding import PartitionSpec as P

R = 2
C = 64
Z = 16
TY = 8
TX = 128
BF = jnp.bfloat16
F32 = jnp.float32
MESH = pl.DeviceIdType.MESH


STEM_PAIRS = 6
INNER_PAIRS = 5
BLOCK_PAIRS = 4
STEM_X = 68
INNER_X = 67
BLOCK_X = 66
XB = 32
AROUND = [(dy, dx) for dy in (-1, 0, 1) for dx in (-1, 0, 1) if (dy, dx) != (0, 0)]


def conv_rows(ref, pair, count, near, far):
    def operand(offsets):
        parts = []
        for offset in offsets:
            for k in range(2):
                part = ref[pair + k, offset % 2, offset // 2 : offset // 2 + count]
                parts.append(part.reshape(count * Z, 2 * C))
        return jnp.concatenate(parts, axis=1)

    row = lax.broadcasted_iota(jnp.int32, (1, Z, 2 * C), 1)
    third = jnp.dot(operand(range(4)), far[...], preferred_element_type=F32)
    out = []
    for qx in range(2):
        both = jnp.dot(operand(range(qx, qx + 3)), near[...], preferred_element_type=F32)
        below = both[:, :128].reshape(count, Z, 128)
        above = third[:, qx * 128 : qx * 128 + 128].reshape(count, Z, 128)
        total = both[:, 128:].reshape(count, Z, 128)
        total += jnp.where(row == 0, 0.0, pltpu.roll(below, 1, axis=1))
        total += jnp.where(row == Z - 1, 0.0, pltpu.roll(above, Z - 1, axis=1))
        out.append(total)
    return out


def build_conv_weights(kernel_ref, near, far):
    zero = jnp.zeros((C, C), BF)

    def band(dz, dx, source):
        blocks = []
        for qy in range(2):
            dy = source - qy
            inside = 0 <= dx < 3 and 0 <= dy < 3
            blocks.append(kernel_ref[(dz * 3 + dy) * 3 + dx] if inside else zero)
        return jnp.concatenate(blocks, axis=1)

    for source in range(4):
        for dx in range(3):
            rows = (dx * 4 + source) * C
            for dz in range(2):
                near[rows : rows + C, dz * 128 : dz * 128 + 128] = band(dz, dx, source)
        for offset in range(4):
            rows = (offset * 4 + source) * C
            for qx in range(2):
                far[rows : rows + C, qx * 128 : qx * 128 + 128] = band(2, offset - qx, source)


def zero_columns(ref, columns):
    for pair in range(ref.shape[0]):
        for x in columns:
            ref[pair, x % 2, x // 2] = jnp.zeros((Z, 2 * C), BF)


def coverage_of(position, length):
    total = jnp.zeros(position.shape, F32)
    for b in range(2 * R + 1):
        source = position - (b - R)
        total += jnp.where((source >= 0) & (source < length), float(R + 1 - abs(b - R)), 0.0)
    return total


def compute_kernel(
    tile_hbm, place_hbm, first_hbm, second_hbm, third_hbm, head_hbm, columns_hbm, blend_hbm,
    out_ref,
    tile_ref, place, first_ref, second, third, head_ref, columns_ref, blend,
    strips, rows_in, sides_in, edge_out, edge_in,
    taps, w1, near2, far2, near3, far3, wh, main, edge, qf, qb, stem, inner, pred, total,
    load_sem, send_sem, recv_sem, edge_send_sem, edge_recv_sem,
):
    gx, gy = lax.axis_index("gx"), lax.axis_index("gy")
    nx, ny = lax.axis_size("gx"), lax.axis_size("gy")
    at_low_x, at_high_x = gx == 0, gx == nx - 1
    at_low_y, at_high_y = gy == 0, gy == ny - 1

    def device(dy, dx):
        return (lax.rem(gx + dx + nx, nx), lax.rem(gy + dy + ny, ny))

    barrier = pltpu.get_barrier_semaphore()
    for dy, dx in AROUND:
        pl.semaphore_signal(barrier, inc=1, device_id=device(dy, dx), device_id_type=MESH)
    loads = []
    for n, (source, target) in enumerate(
        (
            (tile_hbm, tile_ref), (second_hbm, second), (third_hbm, third), (first_hbm, first_ref),
            (place_hbm, place), (head_hbm, head_ref), (columns_hbm, columns_ref), (blend_hbm, blend),
        )
    ):
        loads.append(pltpu.make_async_copy(source, target, load_sem.at[n]))
        loads[-1].start()

    loads[0].wait()
    turned = tile_ref[...].astype(F32).reshape(Z * TY, TX).T
    strips[0] = turned[0:16].astype(BF)
    strips[1] = turned[TX - 16 : TX].astype(BF)
    pl.semaphore_wait(barrier, len(AROUND))
    copies = []
    for n, (dy, dx) in enumerate(AROUND):
        if dx == 0:
            source, target = tile_ref, rows_in.at[0 if dy == 1 else 1]
        else:
            source, target = strips.at[0 if dx == -1 else 1], sides_in.at[1 - dy, 0 if dx == 1 else 1]
        copies.append(
            pltpu.make_async_remote_copy(
                src_ref=source,
                dst_ref=target,
                send_sem=send_sem.at[n],
                recv_sem=recv_sem.at[n],
                device_id=device(dy, dx),
                device_id_type=MESH,
            )
        )
        copies[-1].start()

    for load in loads[1:]:
        load.wait()
    build_conv_weights(second, near2, far2)
    build_conv_weights(third, near3, far3)
    taps[...] = jnp.zeros((32, C), F32)
    for n in range(9):
        taps[3 * n : 3 * n + 3, :] = first_ref[n].astype(F32)
    tap = taps[...].astype(BF)
    nothing = jnp.zeros((32, C), BF)
    spread = jnp.concatenate(
        [jnp.concatenate([tap if i == q else nothing for i in range(4)], axis=1) for q in range(4)], axis=0
    )
    for pair in range(STEM_PAIRS):
        w1[pair] = jnp.dot(place[pair], spread, preferred_element_type=F32).astype(BF)
    for py in range(2):
        wh[py * C : py * C + C, :] = jnp.dot(
            head_ref[...], columns_ref[py], preferred_element_type=F32
        ).astype(BF)

    for copy in copies:
        copy.wait()

    lane8 = lax.broadcasted_iota(jnp.int32, (TY, TX), 1)
    lane128 = lax.broadcasted_iota(jnp.int32, (Z * TY, TX), 1)
    for buffer in (main, edge):
        for half in range(2):
            buffer[half, 0] = jnp.zeros((2 * TY, TX), F32)
            buffer[half, Z + 1] = jnp.zeros((2 * TY, TX), F32)
    right_ok = jnp.where(at_high_x, 0, 64)
    left_ok = jnp.where(at_low_x, 128, 64)
    between = jnp.zeros((TX - 32, Z * TY), F32)
    middles, sideways = [], []
    for ty in range(3):
        left, right = sides_in[ty, 0].astype(F32), sides_in[ty, 1].astype(F32)
        sides = jnp.concatenate([right, between, left], axis=0).T
        sides = jnp.where((lane128 < right_ok) | (lane128 >= left_ok), sides, 0.0)
        middle = (tile_ref[...] if ty == 1 else rows_in[ty // 2]).astype(F32)
        sides = sides.reshape(Z, TY, TX)
        if ty != 1:
            outside = at_low_y if ty == 0 else at_high_y
            middle, sides = jnp.where(outside, 0.0, middle), jnp.where(outside, 0.0, sides)
        middles.append(middle)
        sideways.append(sides)
    row8 = lax.broadcasted_iota(jnp.int32, (1, TY, TX), 1)
    end = lax.broadcasted_iota(jnp.int32, (1, TY, TX), 2) == TX - 1
    for part in range(2):
        if part == 0:
            middle, sides = middles[1], sideways[1]
        else:
            middle = jnp.where(row8 < 4, middles[2], middles[0])
            sides = jnp.where(row8 < 4, sideways[2], sideways[0])
        next_middle, next_sides = pltpu.roll(middle, TX - 1, axis=2), pltpu.roll(sides, TX - 1, axis=2)
        rows = slice(part * TY, part * TY + TY)
        main[0, 1 : Z + 1, rows, :] = middle
        main[1, 1 : Z + 1, rows, :] = jnp.where(end, next_sides, next_middle)
        edge[0, 1 : Z + 1, rows, :] = sides
        edge[1, 1 : Z + 1, rows, :] = jnp.where(end, next_middle, next_sides)
    filler = jnp.zeros((2 * TY, TX), F32)
    for z in range(Z):
        turns = []
        for buffer in (main, edge):
            parts = []
            for half in range(2):
                parts += [buffer[half, z], buffer[half, z + 1], buffer[half, z + 2], filler]
            turns.append(jnp.concatenate(parts, axis=0).T)
        middle, sides = turns
        qf[pl.ds(8 * Z + z, TX, stride=Z), :] = middle
        qf[pl.ds(z, 8, stride=Z), :] = sides[120:128]
        qf[pl.ds(136 * Z + z, 8, stride=Z), :] = sides[0:8]

    for m in range(STEM_X + 1):
        qb[m] = qf[(2 * m + 3) * Z : (2 * m + 4) * Z, :].astype(BF)

    def stem_body(pair, carry):
        parts = [qb[k : k + STEM_X].reshape(STEM_X * Z, 128) for k in range(2)]
        acc = jnp.dot(jnp.concatenate(parts, axis=1), w1[pair], preferred_element_type=F32)
        outside = (at_low_y & (pair == 0)) | (at_high_y & (pair == STEM_PAIRS - 1))
        acc = jnp.maximum(acc, 0.0) * jnp.where(outside, 0.0, 1.0)
        for qx in range(2):
            value = acc[:, qx * 128 : qx * 128 + 128].reshape(STEM_X, Z, 128)
            stem[pair, qx] = value.astype(BF)
        return carry

    lax.fori_loop(0, STEM_PAIRS, stem_body, 0)

    @pl.when(at_low_x)
    def _():
        zero_columns(stem, range(4))

    @pl.when(at_high_x)
    def _():
        zero_columns(stem, range(132, 136))

    upper = (lax.broadcasted_iota(jnp.int32, (1, 1, 128), 2) // C)

    def inner_body(pair, carry):
        sums = conv_rows(stem, pair, INNER_X, near2, far2)
        low = jnp.where(at_low_y & (pair == 0), 0, -1)
        high = jnp.where(at_high_y & (pair == INNER_PAIRS - 1), 1, -1)
        keep = jnp.where((upper == low) | (upper == high), 0.0, 1.0)
        for qx in range(2):
            inner[pair, qx] = (jnp.maximum(sums[qx], 0.0) * keep).astype(BF)
        return carry

    lax.fori_loop(0, INNER_PAIRS, inner_body, 0)

    @pl.when(at_low_x)
    def _():
        zero_columns(inner, range(3))

    @pl.when(at_high_x)
    def _():
        zero_columns(inner, range(131, 134))

    def block_body(pair):
        sums = conv_rows(inner, pair, BLOCK_X, near3, far3)
        for qx in range(2):
            old = stem[pair + 1, qx, 1 : 1 + BLOCK_X].astype(F32)
            value = jnp.maximum(sums[qx] + old, 0.0).astype(BF).reshape(BLOCK_X * Z, 128)
            logits = jnp.dot(value, wh[...], preferred_element_type=F32)
            pred[pair, qx] = jnp.tanh(logits).astype(BF).reshape(BLOCK_X, Z, 256)

        @pl.when(at_low_x)
        def _():
            for parity in range(2):
                pred[pair, parity, 0] = jnp.zeros((Z, 256), BF)

        @pl.when(at_high_x)
        def _():
            for parity in range(2):
                pred[pair, parity, BLOCK_X - 1] = jnp.zeros((Z, 256), BF)

    lanes = lax.broadcasted_iota(jnp.int32, (1, Z, 128), 2)

    def blend_rows(pairs, first, more):
        def body(step, carry):
            j = step * XB
            for qx in range(2):
                operands = []
                for pair in pairs:
                    for half in range(2):
                        chosen = None
                        for n, a in enumerate((0, 1, 2) if half == 0 else (2, 3, 4)):
                            at = qx - a + 4
                            part = pred[pair, at % 2, pl.ds(j + at // 2, XB), :, half * 128 : half * 128 + 128]
                            chosen = part if n == 0 else jnp.where(lanes >= A_START[half][n], part, chosen)
                        operands.append(chosen.reshape(XB * Z, 128))
                added = jnp.dot(
                    jnp.concatenate(operands, axis=1),
                    blend[first : first + 256 * len(pairs), :],
                    preferred_element_type=F32,
                )
                rows = pl.ds(pl.multiple_of(j * Z, XB * Z), XB * Z)
                total[qx, rows, :] = total[qx, rows, :] + added if more else added
            return carry

        lax.fori_loop(0, TX // 2 // XB, body, 0)

    def turned_total(z):
        even = total[0, pl.ds(z, TX // 2, stride=Z), :]
        odd = total[1, pl.ds(z, TX // 2, stride=Z), :]
        return jnp.stack([even, odd], axis=1).reshape(TX, 128).T

    def outer_body(step, carry):
        block_body(step * (BLOCK_PAIRS - 1))
        return carry

    lax.fori_loop(0, 2, outer_body, 0)
    blend_rows((0, BLOCK_PAIRS - 1), 0, False)
    for z in range(Z):
        both = turned_total(z)
        for side in range(2):
            edge_out[side, z] = both[24 + 8 * side : 32 + 8 * side]
    edges = []
    for side, dy in enumerate((-1, 1)):
        edges.append(
            pltpu.make_async_remote_copy(
                src_ref=edge_out.at[side],
                dst_ref=edge_in.at[side],
                send_sem=edge_send_sem.at[side],
                recv_sem=edge_recv_sem.at[side],
                device_id=device(dy, 0),
                device_id_type=MESH,
            )
        )
        edges[-1].start()

    def middle_body(step, carry):
        block_body(step + 1)
        return carry

    lax.fori_loop(0, BLOCK_PAIRS - 2, middle_body, 0)
    blend_rows(tuple(range(1, BLOCK_PAIRS - 1)), 512, True)

    y8 = lax.broadcasted_iota(jnp.int32, (TY, TX), 0)
    scale = 0.5 / (coverage_of(gy * TY + y8, ny * TY) * coverage_of(gx * TX + lane8, nx * TX))
    from_above = (y8 < 2) & (gy > 0)
    from_below = (y8 >= TY - 2) & (gy < ny - 1)
    for copy in edges:
        copy.wait()
    for z in range(Z):
        both = turned_total(z)
        below, above = edge_in[0, z], edge_in[1, z]
        for c in range(3):
            added = both[c * TY : c * TY + TY, :]
            added += jnp.where(from_above, above if c == 0 else pltpu.roll(above, TY - 2 * c, axis=0), 0.0)
            added += jnp.where(from_below, pltpu.roll(below, TY - 2 - 2 * c, axis=0), 0.0)
            out_ref[c, z] = 0.5 + added * scale


def lane_plan():
    plan, starts = [], []
    for half in range(2):
        lanes, begin = [], []
        for a in (0, 1, 2) if half == 0 else (2, 3, 4):
            begin.append(len(lanes))
            for py in range(2):
                if a == 2 and py != half:
                    continue
                lanes += [(a, py, b, c) for b in range(5) for c in range(3)]
        plan.append(lanes)
        starts.append(begin)
    return plan, starts


LANES, A_START = lane_plan()


def constants():
    place = np.zeros((STEM_PAIRS, 4, 64, 128), np.float32)
    for pair in range(STEM_PAIRS):
        for qx in range(2):
            for qy in range(2):
                for dz in range(3):
                    for dy in range(3):
                        for dx in range(3):
                            y = (2 * pair + qy + dy - 3) % 16
                            place[pair, qx + dx, dz * 16 + y, (qx * 2 + qy) * 32 + (dz * 3 + dy) * 3 + dx] = 1
    columns = np.zeros((2, 75, 256), np.float32)
    pairs = (0, BLOCK_PAIRS - 1) + tuple(range(1, BLOCK_PAIRS - 1))
    blend = np.zeros((len(pairs), 256, 128), np.float32)
    for half in range(2):
        for n, (a, py, b, c) in enumerate(LANES[half]):
            columns[py, (a * 5 + b) * 3 + c, half * 128 + n] = 0.5
            for i, pair in enumerate(pairs):
                y = 2 * pair + py + b - R
                if y < 0:
                    lane = 24 + 2 * c + y + R
                elif y >= TY:
                    lane = 32 + 2 * c + y - TY
                else:
                    lane = c * TY + y
                blend[i, half * 128 + n, lane] = (R + 1 - abs(a - R)) * (R + 1 - abs(b - R))
    return (
        jnp.asarray(place.reshape(STEM_PAIRS, 256, 128), BF),
        jnp.asarray(columns, BF),
        jnp.asarray(blend.reshape(-1, 128), BF),
    )


def local(intensity, first_kernel, second_kernel, third_kernel, head_weight):
    place, columns, blend = constants()
    vmem = pl.BlockSpec(memory_space=pltpu.VMEM)
    hbm = pl.BlockSpec(memory_space=pltpu.HBM)
    return pl.pallas_call(
        compute_kernel,
        out_shape=jax.ShapeDtypeStruct((3, Z, TY, TX), F32),
        in_specs=[hbm] * 8,
        out_specs=vmem,
        scratch_shapes=[
            pltpu.VMEM(intensity.shape, BF),
            pltpu.VMEM(place.shape, BF),
            pltpu.VMEM((9, 3, C), BF),
            pltpu.VMEM((27, C, C), BF),
            pltpu.VMEM((27, C, C), BF),
            pltpu.VMEM(head_weight.shape, BF),
            pltpu.VMEM(columns.shape, BF),
            pltpu.VMEM(blend.shape, BF),
            pltpu.VMEM((2, 16, Z * TY), BF),
            pltpu.VMEM((2, Z, TY, TX), BF),
            pltpu.VMEM((3, 2, 16, Z * TY), BF),
            pltpu.VMEM((2, Z, TY, TX), F32),
            pltpu.VMEM((2, Z, TY, TX), F32),
            pltpu.VMEM((32, C), F32),
            pltpu.VMEM((STEM_PAIRS, 256, 256), BF),
            pltpu.VMEM((768, 256), BF),
            pltpu.VMEM((1024, 256), BF),
            pltpu.VMEM((768, 256), BF),
            pltpu.VMEM((1024, 256), BF),
            pltpu.VMEM((128, 256), BF),
            pltpu.VMEM((2, Z + 2, 2 * TY, TX), F32),
            pltpu.VMEM((2, Z + 2, 2 * TY, TX), F32),
            pltpu.VMEM((144 * Z, 128), F32),
            pltpu.VMEM((STEM_X + 1, Z, 128), BF),
            pltpu.VMEM((STEM_PAIRS, 2, STEM_X, Z, 128), BF),
            pltpu.VMEM((INNER_PAIRS, 2, INNER_X, Z, 128), BF),
            pltpu.VMEM((BLOCK_PAIRS, 2, BLOCK_X, Z, 256), BF),
            pltpu.VMEM((2, TX // 2 * Z, 128), F32),
            pltpu.SemaphoreType.DMA((8,)),
            pltpu.SemaphoreType.DMA((8,)),
            pltpu.SemaphoreType.DMA((8,)),
            pltpu.SemaphoreType.DMA((2,)),
            pltpu.SemaphoreType.DMA((2,)),
        ],
        compiler_params=pltpu.CompilerParams(
            collective_id=0, has_side_effects=True, vmem_limit_bytes=56 * 2**20
        ),
        name="convnet",
    )(
        intensity, place, first_kernel.reshape(9, 3, C),
        second_kernel.reshape(27, C, C), third_kernel.reshape(27, C, C), head_weight, columns, blend,
    )


def solution(mesh):
    in_specs = (P(None, "gy", "gx"), P(), P(), P(), P())
    out_specs = P(None, None, "gy", "gx")
    return jax.shard_map(local, mesh=mesh, in_specs=in_specs, out_specs=out_specs, check_vma=False)
```

time: 46.3 us -> 37.8 us (0.82)
  Pallas kernels: 44.5 us -> 36 us
    pallas_call x1, Pallas kernels: 44.5 us -> 36 us  [local(): pl.pallas_call(compute_kernel, out_shape=jax.ShapeDtypeStruct((3, Z, TY,...]
where the time goes in v3:
time: 37.8 us; the launch traced here: 37.7 us
  Pallas kernels  36 us (95%)
  local copies, waits for them, and re-layouts  1.62 us (4%)
    pallas_call x1, Pallas kernels, local(): pl.pallas_call(compute_kernel, out_shape=jax.ShapeDtypeStruct((3, Z, TY,...  36 us
    unnamed x1, local copies, waits for them, and re-layouts  1.62 us

profile of v3, /device:TPU:1, one launch (start us, length us, event | category | flops | bytes accessed | tf_op | source)
XLA Modules:
  0.0 37.7 jit_solution(17414875205968104162)
XLA Ops:
  0.0 36.0 %convnet.1 = f32[3,16,8,128]{3,2,1,0:T(8,128)} custom-call(bf16[16,8,128]{2,1,0:T(8,128)(2,1)} %tile_hbm.1, bf16[6,256,128]{2,1,0:T(8,128)(2,1)} %constant.6.clone.place_hbm, bf16[9,3,64]{2,1,0:T(4,128)(2,1)} %bitcast.5, bf16[27,64,64]{2,1,0:T(8,128)(2,1)} %bitcast.3, bf16[27,64,64]{2,1,0:T(8,128)(2,1)} %bitcast.4, bf16[64,75]{1,0:T(8,128)(2,1)} %head_hbm.1, ...), custom_call_target="tpu_custom_call" | custom-call | tf_op jit(solution)/shard_map/convnet/pallas_call | solution.py:406
  36.1 1.6 %copy.10 = f32[3,16,8,128]{3,2,1,0:T(8,128)} copy(f32[3,16,8,128]{3,2,1,0:T(8,128)} %convnet.1) | data formatting | bytes 393216

commit v4 on v3

--- a/solution.py
+++ b/solution.py
@@ -25,15 +25,24 @@
 INNER_X = 67
 BLOCK_X = 66
 XB = 32
+STEM_OWN, STEM_SIDES = ((3, 65),), ((0, 3), (65, STEM_X))
+INNER_OWN, INNER_SIDES = ((3, 64),), ((0, 3), (64, INNER_X))
 AROUND = [(dy, dx) for dy in (-1, 0, 1) for dx in (-1, 0, 1) if (dy, dx) != (0, 0)]
 
 
-def conv_rows(ref, pair, count, near, far):
+def join(parts):
+    return parts[0] if len(parts) == 1 else jnp.concatenate(parts, axis=0)
+
+
+def conv_rows(ref, pair, spans, near, far):
+    count = sum(end - begin for begin, end in spans)
+
     def operand(offsets):
         parts = []
         for offset in offsets:
             for k in range(2):
-                part = ref[pair + k, offset % 2, offset // 2 : offset // 2 + count]
+                at = offset // 2
+                part = join([ref[pair + k, offset % 2, begin + at : end + at] for begin, end in spans])
                 parts.append(part.reshape(count * Z, 2 * C))
         return jnp.concatenate(parts, axis=1)
 
@@ -158,15 +167,73 @@
             head_ref[...], columns_ref[py], preferred_element_type=F32
         ).astype(BF)
 
-    for copy in copies:
-        copy.wait()
-
     lane8 = lax.broadcasted_iota(jnp.int32, (TY, TX), 1)
     lane128 = lax.broadcasted_iota(jnp.int32, (Z * TY, TX), 1)
+    end = lax.broadcasted_iota(jnp.int32, (1, TY, TX), 2) == TX - 1
     for buffer in (main, edge):
         for half in range(2):
             buffer[half, 0] = jnp.zeros((2 * TY, TX), F32)
             buffer[half, Z + 1] = jnp.zeros((2 * TY, TX), F32)
+    filler = jnp.zeros((2 * TY, TX), F32)
+
+    def turn(buffer, z):
+        parts = []
+        for half in range(2):
+            parts += [buffer[half, z], buffer[half, z + 1], buffer[half, z + 2], filler]
+        return jnp.concatenate(parts, axis=0).T
+
+    own = tile_ref[...].astype(F32)
+    main[0, 1 : Z + 1, 0:TY, :] = own
+    main[1, 1 : Z + 1, 0:TY, :] = jnp.where(end, 0.0, pltpu.roll(own, TX - 1, axis=2))
+    for half in range(2):
+        main[half, 1 : Z + 1, TY : 2 * TY, :] = jnp.zeros((Z, TY, TX), F32)
+    for z in range(Z):
+        qf[pl.ds(8 * Z + z, TX, stride=Z), :] = turn(main, z)
+    for m in range(3, STEM_X - 2):
+        qb[m] = qf[(2 * m + 3) * Z : (2 * m + 4) * Z, :].astype(BF)
+
+    def stem_rows(pair, spans):
+        parts = []
+        for k in range(2):
+            part = join([qb[begin + k : end + k] for begin, end in spans])
+            parts.append(part.reshape(-1, 128))
+        acc = jnp.dot(jnp.concatenate(parts, axis=1), w1[pair], preferred_element_type=F32)
+        outside = (at_low_y & (pair == 0)) | (at_high_y & (pair == STEM_PAIRS - 1))
+        acc = jnp.maximum(acc, 0.0) * jnp.where(outside, 0.0, 1.0)
+        for qx in range(2):
+            value = acc[:, qx * 128 : qx * 128 + 128].astype(BF).reshape(-1, Z, 128)
+            at = 0
+            for begin, end in spans:
+                stem[pair, qx, begin:end] = value[at : at + end - begin]
+                at += end - begin
+
+    upper = lax.broadcasted_iota(jnp.int32, (1, 1, 128), 2) // C
+
+    def inner_rows(pair, spans):
+        sums = conv_rows(stem, pair, spans, near2, far2)
+        low = jnp.where(at_low_y & (pair == 0), 0, -1)
+        high = jnp.where(at_high_y & (pair == INNER_PAIRS - 1), 1, -1)
+        keep = jnp.where((upper == low) | (upper == high), 0.0, 1.0)
+        for qx in range(2):
+            value = (jnp.maximum(sums[qx], 0.0) * keep).astype(BF)
+            at = 0
+            for begin, end in spans:
+                inner[pair, qx, begin:end] = value[at : at + end - begin]
+                at += end - begin
+
+    def loop(count, pair_of, body):
+        def step(n, carry):
+            body(pair_of(n))
+            return carry
+
+        lax.fori_loop(0, count, step, 0)
+
+    loop(2, lambda n: n + 2, lambda pair: stem_rows(pair, STEM_OWN))
+    inner_rows(2, INNER_OWN)
+
+    for copy in copies:
+        copy.wait()
+
     right_ok = jnp.where(at_high_x, 0, 64)
     left_ok = jnp.where(at_low_x, 128, 64)
     between = jnp.zeros((TX - 32, Z * TY), F32)
@@ -175,15 +242,14 @@
         left, right = sides_in[ty, 0].astype(F32), sides_in[ty, 1].astype(F32)
         sides = jnp.concatenate([right, between, left], axis=0).T
         sides = jnp.where((lane128 < right_ok) | (lane128 >= left_ok), sides, 0.0)
-        middle = (tile_ref[...] if ty == 1 else rows_in[ty // 2]).astype(F32)
         sides = sides.reshape(Z, TY, TX)
+        middle = own if ty == 1 else rows_in[ty // 2].astype(F32)
         if ty != 1:
             outside = at_low_y if ty == 0 else at_high_y
             middle, sides = jnp.where(outside, 0.0, middle), jnp.where(outside, 0.0, sides)
         middles.append(middle)
         sideways.append(sides)
     row8 = lax.broadcasted_iota(jnp.int32, (1, TY, TX), 1)
-    end = lax.broadcasted_iota(jnp.int32, (1, TY, TX), 2) == TX - 1
     for part in range(2):
         if part == 0:
             middle, sides = middles[1], sideways[1]
@@ -196,33 +262,16 @@
         main[1, 1 : Z + 1, rows, :] = jnp.where(end, next_sides, next_middle)
         edge[0, 1 : Z + 1, rows, :] = sides
         edge[1, 1 : Z + 1, rows, :] = jnp.where(end, next_middle, next_sides)
-    filler = jnp.zeros((2 * TY, TX), F32)
     for z in range(Z):
-        turns = []
-        for buffer in (main, edge):
-            parts = []
-            for half in range(2):
-                parts += [buffer[half, z], buffer[half, z + 1], buffer[half, z + 2], filler]
-            turns.append(jnp.concatenate(parts, axis=0).T)
-        middle, sides = turns
-        qf[pl.ds(8 * Z + z, TX, stride=Z), :] = middle
+        sides = turn(edge, z)
+        qf[pl.ds(8 * Z + z, TX, stride=Z), :] = turn(main, z)
         qf[pl.ds(z, 8, stride=Z), :] = sides[120:128]
         qf[pl.ds(136 * Z + z, 8, stride=Z), :] = sides[0:8]
-
     for m in range(STEM_X + 1):
         qb[m] = qf[(2 * m + 3) * Z : (2 * m + 4) * Z, :].astype(BF)
 
-    def stem_body(pair, carry):
-        parts = [qb[k : k + STEM_X].reshape(STEM_X * Z, 128) for k in range(2)]
-        acc = jnp.dot(jnp.concatenate(parts, axis=1), w1[pair], preferred_element_type=F32)
-        outside = (at_low_y & (pair == 0)) | (at_high_y & (pair == STEM_PAIRS - 1))
-        acc = jnp.maximum(acc, 0.0) * jnp.where(outside, 0.0, 1.0)
-        for qx in range(2):
-            value = acc[:, qx * 128 : qx * 128 + 128].reshape(STEM_X, Z, 128)
-            stem[pair, qx] = value.astype(BF)
-        return carry
-
-    lax.fori_loop(0, STEM_PAIRS, stem_body, 0)
+    loop(4, lambda n: n + n // 2 * 2, lambda pair: stem_rows(pair, ((0, STEM_X),)))
+    loop(2, lambda n: n + 2, lambda pair: stem_rows(pair, STEM_SIDES))
 
     @pl.when(at_low_x)
     def _():
@@ -232,18 +281,8 @@
     def _():
         zero_columns(stem, range(132, 136))
 
-    upper = (lax.broadcasted_iota(jnp.int32, (1, 1, 128), 2) // C)
-
-    def inner_body(pair, carry):
-        sums = conv_rows(stem, pair, INNER_X, near2, far2)
-        low = jnp.where(at_low_y & (pair == 0), 0, -1)
-        high = jnp.where(at_high_y & (pair == INNER_PAIRS - 1), 1, -1)
-        keep = jnp.where((upper == low) | (upper == high), 0.0, 1.0)
-        for qx in range(2):
-            inner[pair, qx] = (jnp.maximum(sums[qx], 0.0) * keep).astype(BF)
-        return carry
-
-    lax.fori_loop(0, INNER_PAIRS, inner_body, 0)
+    loop(4, lambda n: n + n // 2, lambda pair: inner_rows(pair, ((0, INNER_X),)))
+    inner_rows(2, INNER_SIDES)
 
     @pl.when(at_low_x)
     def _():
@@ -254,7 +293,7 @@
         zero_columns(inner, range(131, 134))
 
     def block_body(pair):
-        sums = conv_rows(inner, pair, BLOCK_X, near3, far3)
+        sums = conv_rows(inner, pair, ((0, BLOCK_X),), near3, far3)
         for qx in range(2):
             old = stem[pair + 1, qx, 1 : 1 + BLOCK_X].astype(F32)
             value = jnp.maximum(sums[qx] + old, 0.0).astype(BF).reshape(BLOCK_X * Z, 128)
@@ -291,16 +330,15 @@
                     blend[first : first + 256 * len(pairs), :],
                     preferred_element_type=F32,
                 )
-                rows = pl.ds(pl.multiple_of(j * Z, XB * Z), XB * Z)
-                total[qx, rows, :] = total[qx, rows, :] + added if more else added
+                added = added.reshape(XB, Z, 128)
+                at = pl.ds(j, XB)
+                total[at, qx] = total[at, qx] + added if more else added
             return carry
 
         lax.fori_loop(0, TX // 2 // XB, body, 0)
 
     def turned_total(z):
-        even = total[0, pl.ds(z, TX // 2, stride=Z), :]
-        odd = total[1, pl.ds(z, TX // 2, stride=Z), :]
-        return jnp.stack([even, odd], axis=1).reshape(TX, 128).T
+        return total.reshape(TX * Z, 128)[pl.ds(z, TX, stride=Z), :].T
 
     def outer_body(step, carry):
         block_body(step * (BLOCK_PAIRS - 1))
@@ -436,7 +474,7 @@
             pltpu.VMEM((STEM_PAIRS, 2, STEM_X, Z, 128), BF),
             pltpu.VMEM((INNER_PAIRS, 2, INNER_X, Z, 128), BF),
             pltpu.VMEM((BLOCK_PAIRS, 2, BLOCK_X, Z, 256), BF),
-            pltpu.VMEM((2, TX // 2 * Z, 128), F32),
+            pltpu.VMEM((TX // 2, 2, Z, 128), F32),
             pltpu.SemaphoreType.DMA((8,)),
             pltpu.SemaphoreType.DMA((8,)),
             pltpu.SemaphoreType.DMA((8,)),

time: 37.8 us -> 35.2 us (0.931)
  Pallas kernels: 36 us -> 33.5 us
    pallas_call x1, Pallas kernels: 36 us -> 33.5 us  [local(): pl.pallas_call(compute_kernel, out_shape=jax.ShapeDtypeStruct((3, Z, TY,...]
where the time goes in v4:
time: 35.2 us; the launch traced here: 35.1 us
  Pallas kernels  33.5 us (95%)
  local copies, waits for them, and re-layouts  1.62 us (5%)
    pallas_call x1, Pallas kernels, local(): pl.pallas_call(compute_kernel, out_shape=jax.ShapeDtypeStruct((3, Z, TY,...  33.5 us
    unnamed x1, local copies, waits for them, and re-layouts  1.62 us

profile of v4, /device:TPU:1, one launch (start us, length us, event | category | flops | bytes accessed | tf_op | source)
XLA Modules:
  0.0 35.1 jit_solution(5439770485747225400)
XLA Ops:
  0.0 33.5 %convnet.1 = f32[3,16,8,128]{3,2,1,0:T(8,128)} custom-call(bf16[16,8,128]{2,1,0:T(8,128)(2,1)} %tile_hbm.1, bf16[6,256,128]{2,1,0:T(8,128)(2,1)} %constant.6.clone.place_hbm, bf16[9,3,64]{2,1,0:T(4,128)(2,1)} %bitcast.5, bf16[27,64,64]{2,1,0:T(8,128)(2,1)} %bitcast.3, bf16[27,64,64]{2,1,0:T(8,128)(2,1)} %bitcast.4, bf16[64,75]{1,0:T(8,128)(2,1)} %head_hbm.1, ...), custom_call_target="tpu_custom_call" | custom-call | tf_op jit(solution)/shard_map/convnet/pallas_call | solution.py:444
  33.5 1.6 %copy.10 = f32[3,16,8,128]{3,2,1,0:T(8,128)} copy(f32[3,16,8,128]{3,2,1,0:T(8,128)} %convnet.1) | data formatting | bytes 393216

commit v5 on v4

--- a/solution.py
+++ b/solution.py
@@ -112,9 +112,21 @@
     def device(dy, dx):
         return (lax.rem(gx + dx + nx, nx), lax.rem(gy + dy + ny, ny))
 
+    def inside(dy, dx):
+        found = None
+        for step, low, high in ((dy, at_low_y, at_high_y), (dx, at_low_x, at_high_x)):
+            if step:
+                here = jnp.logical_not(low if step < 0 else high)
+                found = here if found is None else found & here
+        return found
+
     barrier = pltpu.get_barrier_semaphore()
     for dy, dx in AROUND:
-        pl.semaphore_signal(barrier, inc=1, device_id=device(dy, dx), device_id_type=MESH)
+
+        @pl.when(inside(dy, dx))
+        def _():
+            pl.semaphore_signal(barrier, inc=1, device_id=device(dy, dx), device_id_type=MESH)
+
     loads = []
     for n, (source, target) in enumerate(
         (
@@ -129,7 +141,9 @@
     turned = tile_ref[...].astype(F32).reshape(Z * TY, TX).T
     strips[0] = turned[0:16].astype(BF)
     strips[1] = turned[TX - 16 : TX].astype(BF)
-    pl.semaphore_wait(barrier, len(AROUND))
+    beside_y = 2 - at_low_y.astype(jnp.int32) - at_high_y.astype(jnp.int32)
+    beside_x = 2 - at_low_x.astype(jnp.int32) - at_high_x.astype(jnp.int32)
+    pl.semaphore_wait(barrier, (beside_y + 1) * (beside_x + 1) - 1)
     copies = []
     for n, (dy, dx) in enumerate(AROUND):
         if dx == 0:
@@ -146,7 +160,7 @@
                 device_id_type=MESH,
             )
         )
-        copies[-1].start()
+        pl.when(inside(dy, dx))(copies[-1].start)
 
     for load in loads[1:]:
         load.wait()
@@ -231,8 +245,9 @@
     loop(2, lambda n: n + 2, lambda pair: stem_rows(pair, STEM_OWN))
     inner_rows(2, INNER_OWN)
 
-    for copy in copies:
-        copy.wait()
+    for copy, (dy, dx) in zip(copies, AROUND):
+        pl.when(inside(dy, dx))(copy.wait_send)
+        pl.when(inside(-dy, -dx))(copy.wait_recv)
 
     right_ok = jnp.where(at_high_x, 0, 64)
     left_ok = jnp.where(at_low_x, 128, 64)
@@ -362,7 +377,7 @@
                 device_id_type=MESH,
             )
         )
-        edges[-1].start()
+        pl.when(inside(dy, 0))(edges[-1].start)
 
     def middle_body(step, carry):
         block_body(step + 1)
@@ -375,8 +390,9 @@
     scale = 0.5 / (coverage_of(gy * TY + y8, ny * TY) * coverage_of(gx * TX + lane8, nx * TX))
     from_above = (y8 < 2) & (gy > 0)
     from_below = (y8 >= TY - 2) & (gy < ny - 1)
-    for copy in edges:
-        copy.wait()
+    for copy, dy in zip(edges, (-1, 1)):
+        pl.when(inside(dy, 0))(copy.wait_send)
+        pl.when(inside(-dy, 0))(copy.wait_recv)
     for z in range(Z):
         both = turned_total(z)
         below, above = edge_in[0, z], edge_in[1, z]

time: 35.2 us -> 30.5 us (0.87)
  Pallas kernels: 33.5 us -> 28.8 us
    pallas_call x1, Pallas kernels: 33.5 us -> 28.8 us  [local(): pl.pallas_call(compute_kernel, out_shape=jax.ShapeDtypeStruct((3, Z, TY,...]
where the time goes in v5:
time: 30.5 us; the launch traced here: 30.4 us
  Pallas kernels  28.8 us (94%)
  local copies, waits for them, and re-layouts  1.62 us (5%)
    pallas_call x1, Pallas kernels, local(): pl.pallas_call(compute_kernel, out_shape=jax.ShapeDtypeStruct((3, Z, TY,...  28.8 us
    unnamed x1, local copies, waits for them, and re-layouts  1.62 us

profile of v5, /device:TPU:1, one launch (start us, length us, event | category | flops | bytes accessed | tf_op | source)
XLA Modules:
  0.0 30.4 jit_solution(4938760189772027313)
XLA Ops:
  0.0 28.8 %convnet.1 = f32[3,16,8,128]{3,2,1,0:T(8,128)} custom-call(bf16[16,8,128]{2,1,0:T(8,128)(2,1)} %tile_hbm.1, bf16[6,256,128]{2,1,0:T(8,128)(2,1)} %constant.6.clone.place_hbm, bf16[9,3,64]{2,1,0:T(4,128)(2,1)} %bitcast.5, bf16[27,64,64]{2,1,0:T(8,128)(2,1)} %bitcast.3, bf16[27,64,64]{2,1,0:T(8,128)(2,1)} %bitcast.4, bf16[64,75]{1,0:T(8,128)(2,1)} %head_hbm.1, ...), custom_call_target="tpu_custom_call" | custom-call | tf_op jit(solution)/shard_map/convnet/pallas_call | solution.py:460
  28.8 1.6 %copy.10 = f32[3,16,8,128]{3,2,1,0:T(8,128)} copy(f32[3,16,8,128]{3,2,1,0:T(8,128)} %convnet.1) | data formatting | bytes 393216

commit v6 on v5

--- a/solution.py
+++ b/solution.py
@@ -24,7 +24,7 @@
 STEM_X = 68
 INNER_X = 67
 BLOCK_X = 66
-XB = 32
+XB = 64
 STEM_OWN, STEM_SIDES = ((3, 65),), ((0, 3), (65, STEM_X))
 INNER_OWN, INNER_SIDES = ((3, 64),), ((0, 3), (64, INNER_X))
 AROUND = [(dy, dx) for dy in (-1, 0, 1) for dx in (-1, 0, 1) if (dy, dx) != (0, 0)]
@@ -240,7 +240,7 @@
             body(pair_of(n))
             return carry
 
-        lax.fori_loop(0, count, step, 0)
+        lax.fori_loop(0, count, step, 0, unroll=True)
 
     loop(2, lambda n: n + 2, lambda pair: stem_rows(pair, STEM_OWN))
     inner_rows(2, INNER_OWN)

time: 30.5 us -> 29 us (0.951)
  Pallas kernels: 28.8 us -> 27.3 us
    pallas_call x1, Pallas kernels: 28.8 us -> 27.3 us  [local(): pl.pallas_call(compute_kernel, out_shape=jax.ShapeDtypeStruct((3, Z, TY,...]
where the time goes in v6:
time: 29 us; the launch traced here: 28.9 us
  Pallas kernels  27.3 us (94%)
  local copies, waits for them, and re-layouts  1.62 us (6%)
    pallas_call x1, Pallas kernels, local(): pl.pallas_call(compute_kernel, out_shape=jax.ShapeDtypeStruct((3, Z, TY,...  27.3 us
    unnamed x1, local copies, waits for them, and re-layouts  1.62 us

profile of v6, /device:TPU:1, one launch (start us, length us, event | category | flops | bytes accessed | tf_op | source)
XLA Modules:
  0.0 28.9 jit_solution(2477172041877307042)
XLA Ops:
  0.0 27.3 %convnet.1 = f32[3,16,8,128]{3,2,1,0:T(8,128)} custom-call(bf16[16,8,128]{2,1,0:T(8,128)(2,1)} %tile_hbm.1, bf16[6,256,128]{2,1,0:T(8,128)(2,1)} %constant.6.clone.place_hbm, bf16[9,3,64]{2,1,0:T(4,128)(2,1)} %bitcast.5, bf16[27,64,64]{2,1,0:T(8,128)(2,1)} %bitcast.3, bf16[27,64,64]{2,1,0:T(8,128)(2,1)} %bitcast.4, bf16[64,75]{1,0:T(8,128)(2,1)} %head_hbm.1, ...), custom_call_target="tpu_custom_call" | custom-call | tf_op jit(solution)/shard_map/convnet/pallas_call | solution.py:460
  27.3 1.6 %copy.10 = f32[3,16,8,128]{3,2,1,0:T(8,128)} copy(f32[3,16,8,128]{3,2,1,0:T(8,128)} %convnet.1) | data formatting | bytes 393216

commit v7 on v6

--- a/solution.py
+++ b/solution.py
@@ -459,7 +459,7 @@
     hbm = pl.BlockSpec(memory_space=pltpu.HBM)
     return pl.pallas_call(
         compute_kernel,
-        out_shape=jax.ShapeDtypeStruct((3, Z, TY, TX), F32),
+        out_shape=pltpu.VMEM((3, Z, TY, TX), F32),
         in_specs=[hbm] * 8,
         out_specs=vmem,
         scratch_shapes=[

time: 29 us -> 27.4 us (0.945)
  local copies, waits for them, and re-layouts: 1.62 us -> 0.68 us
  Pallas kernels: 27.3 us -> 26.6 us
    unnamed x1, local copies, waits for them, and re-layouts: 1.62 us -> 0.68 us
    pallas_call x1, Pallas kernels: 27.3 us -> 26.6 us  [local(): pl.pallas_call(compute_kernel, out_shape=pltpu.VMEM((3, Z, TY, TX), F32),...]
where the time goes in v7:
time: 27.4 us; the launch traced here: 27.3 us
  Pallas kernels  26.6 us (97%)
  local copies, waits for them, and re-layouts  0.68 us (2%)
    pallas_call x1, Pallas kernels, local(): pl.pallas_call(compute_kernel, out_shape=pltpu.VMEM((3, Z, TY, TX), F32),...  26.6 us
    unnamed x1, local copies, waits for them, and re-layouts  0.68 us

profile of v7, /device:TPU:1, one launch (start us, length us, event | category | flops | bytes accessed | tf_op | source)
XLA Modules:
  0.0 27.3 jit_solution(12651365188809525728)
XLA Ops:
  0.0 26.6 %convnet.1 = f32[3,16,8,128]{3,2,1,0:T(8,128)S(1)} custom-call(bf16[16,8,128]{2,1,0:T(8,128)(2,1)} %tile_hbm.1, bf16[6,256,128]{2,1,0:T(8,128)(2,1)} %constant.6.clone.place_hbm, bf16[9,3,64]{2,1,0:T(4,128)(2,1)} %bitcast.5, bf16[27,64,64]{2,1,0:T(8,128)(2,1)} %bitcast.3, bf16[27,64,64]{2,1,0:T(8,128)(2,1)} %bitcast.4, bf16[64,75]{1,0:T(8,128)(2,1)} %head_hbm.1, ...), custom_call_target="tpu_custom_call" | custom-call | tf_op jit(solution)/shard_map/convnet/pallas_call | solution.py:460
  26.6 0.7 %copy.10 = f32[3,16,8,128]{3,2,1,0:T(8,128)} copy(f32[3,16,8,128]{3,2,1,0:T(8,128)S(1)} %convnet.1) | data formatting | bytes 393216

commit v8 on v7

--- a/solution.py
+++ b/solution.py
@@ -34,15 +34,15 @@
     return parts[0] if len(parts) == 1 else jnp.concatenate(parts, axis=0)
 
 
-def conv_rows(ref, pair, spans, near, far):
-    count = sum(end - begin for begin, end in spans)
+def conv_rows(ref, spans, near, far):
+    count = sum(end - begin for _, begin, end in spans)
 
     def operand(offsets):
         parts = []
         for offset in offsets:
             for k in range(2):
                 at = offset // 2
-                part = join([ref[pair + k, offset % 2, begin + at : end + at] for begin, end in spans])
+                part = join([ref[pair + k, offset % 2, begin + at : end + at] for pair, begin, end in spans])
                 parts.append(part.reshape(count * Z, 2 * C))
         return jnp.concatenate(parts, axis=1)
 
@@ -175,7 +175,10 @@
         [jnp.concatenate([tap if i == q else nothing for i in range(4)], axis=1) for q in range(4)], axis=0
     )
     for pair in range(STEM_PAIRS):
-        w1[pair] = jnp.dot(place[pair], spread, preferred_element_type=F32).astype(BF)
+        taken = jnp.dot(place[pair], spread, preferred_element_type=F32)
+        if pair in (0, STEM_PAIRS - 1):
+            taken = taken * jnp.where(at_low_y if pair == 0 else at_high_y, 0.0, 1.0)
+        w1[pair] = taken.astype(BF)
     for py in range(2):
         wh[py * C : py * C + C, :] = jnp.dot(
             head_ref[...], columns_ref[py], preferred_element_type=F32
@@ -212,8 +215,7 @@
             part = join([qb[begin + k : end + k] for begin, end in spans])
             parts.append(part.reshape(-1, 128))
         acc = jnp.dot(jnp.concatenate(parts, axis=1), w1[pair], preferred_element_type=F32)
-        outside = (at_low_y & (pair == 0)) | (at_high_y & (pair == STEM_PAIRS - 1))
-        acc = jnp.maximum(acc, 0.0) * jnp.where(outside, 0.0, 1.0)
+        acc = jnp.maximum(acc, 0.0)
         for qx in range(2):
             value = acc[:, qx * 128 : qx * 128 + 128].astype(BF).reshape(-1, Z, 128)
             at = 0
@@ -223,27 +225,26 @@
 
     upper = lax.broadcasted_iota(jnp.int32, (1, 1, 128), 2) // C
 
-    def inner_rows(pair, spans):
-        sums = conv_rows(stem, pair, spans, near2, far2)
-        low = jnp.where(at_low_y & (pair == 0), 0, -1)
-        high = jnp.where(at_high_y & (pair == INNER_PAIRS - 1), 1, -1)
-        keep = jnp.where((upper == low) | (upper == high), 0.0, 1.0)
+    def inner_rows(spans):
+        sums = conv_rows(stem, spans, near2, far2)
         for qx in range(2):
-            value = (jnp.maximum(sums[qx], 0.0) * keep).astype(BF)
+            value = jnp.maximum(sums[qx], 0.0)
             at = 0
-            for begin, end in spans:
-                inner[pair, qx, begin:end] = value[at : at + end - begin]
+            for pair, begin, end in spans:
+                part = value[at : at + end - begin]
+                if pair == 0:
+                    part = part * jnp.where(upper == jnp.where(at_low_y, 0, -1), 0.0, 1.0)
+                if pair == INNER_PAIRS - 1:
+                    part = part * jnp.where(upper == jnp.where(at_high_y, 1, -1), 0.0, 1.0)
+                inner[pair, qx, begin:end] = part.astype(BF)
                 at += end - begin
 
     def loop(count, pair_of, body):
-        def step(n, carry):
+        for n in range(count):
             body(pair_of(n))
-            return carry
-
-        lax.fori_loop(0, count, step, 0, unroll=True)
 
     loop(2, lambda n: n + 2, lambda pair: stem_rows(pair, STEM_OWN))
-    inner_rows(2, INNER_OWN)
+    inner_rows([(2, begin, end) for begin, end in INNER_OWN])
 
     for copy, (dy, dx) in zip(copies, AROUND):
         pl.when(inside(dy, dx))(copy.wait_send)
@@ -296,8 +297,9 @@
     def _():
         zero_columns(stem, range(132, 136))
 
-    loop(4, lambda n: n + n // 2, lambda pair: inner_rows(pair, ((0, INNER_X),)))
-    inner_rows(2, INNER_SIDES)
+    for pair in (0, 1, 3):
+        inner_rows([(pair, 0, INNER_X)])
+    inner_rows([(4, 0, INNER_X)] + [(2, begin, end) for begin, end in INNER_SIDES])
 
     @pl.when(at_low_x)
     def _():
@@ -308,7 +310,7 @@
         zero_columns(inner, range(131, 134))
 
     def block_body(pair):
-        sums = conv_rows(inner, pair, ((0, BLOCK_X),), near3, far3)
+        sums = conv_rows(inner, [(pair, 0, BLOCK_X)], near3, far3)
         for qx in range(2):
             old = stem[pair + 1, qx, 1 : 1 + BLOCK_X].astype(F32)
             value = jnp.maximum(sums[qx] + old, 0.0).astype(BF).reshape(BLOCK_X * Z, 128)
@@ -353,7 +355,7 @@
         lax.fori_loop(0, TX // 2 // XB, body, 0)
 
     def turned_total(z):
-        return total.reshape(TX * Z, 128)[pl.ds(z, TX, stride=Z), :].T
+        return total.reshape(TX * Z, 128)[pl.ds(z, TX, stride=Z), :][:, :40].T
 
     def outer_body(step, carry):
         block_body(step * (BLOCK_PAIRS - 1))

time: 27.4 us -> 27.3 us (level)
  no operation moved by 1% of the time
where the time goes in v8:
time: 27.3 us; the launch traced here: 27.2 us
  Pallas kernels  26.5 us (97%)
  local copies, waits for them, and re-layouts  0.68 us (2%)
    pallas_call x1, Pallas kernels, local(): pl.pallas_call(compute_kernel, out_shape=pltpu.VMEM((3, Z, TY, TX), F32),...  26.5 us
    unnamed x1, local copies, waits for them, and re-layouts  0.68 us

profile of v8, /device:TPU:1, one launch (start us, length us, event | category | flops | bytes accessed | tf_op | source)
XLA Modules:
  0.0 27.2 jit_solution(121543129221004017)
XLA Ops:
  0.0 26.5 %convnet.1 = f32[3,16,8,128]{3,2,1,0:T(8,128)S(1)} custom-call(bf16[16,8,128]{2,1,0:T(8,128)(2,1)} %tile_hbm.1, bf16[6,256,128]{2,1,0:T(8,128)(2,1)} %constant.6.clone.place_hbm, bf16[9,3,64]{2,1,0:T(4,128)(2,1)} %bitcast.5, bf16[27,64,64]{2,1,0:T(8,128)(2,1)} %bitcast.3, bf16[27,64,64]{2,1,0:T(8,128)(2,1)} %bitcast.4, bf16[64,75]{1,0:T(8,128)(2,1)} %head_hbm.1, ...), custom_call_target="tpu_custom_call" | custom-call | tf_op jit(solution)/shard_map/convnet/pallas_call | solution.py:462
  26.5 0.7 %copy.10 = f32[3,16,8,128]{3,2,1,0:T(8,128)} copy(f32[3,16,8,128]{3,2,1,0:T(8,128)S(1)} %convnet.1) | data formatting | bytes 393216

commit v9 on v8

--- a/solution.py
+++ b/solution.py
@@ -141,27 +141,6 @@
     turned = tile_ref[...].astype(F32).reshape(Z * TY, TX).T
     strips[0] = turned[0:16].astype(BF)
     strips[1] = turned[TX - 16 : TX].astype(BF)
-    beside_y = 2 - at_low_y.astype(jnp.int32) - at_high_y.astype(jnp.int32)
-    beside_x = 2 - at_low_x.astype(jnp.int32) - at_high_x.astype(jnp.int32)
-    pl.semaphore_wait(barrier, (beside_y + 1) * (beside_x + 1) - 1)
-    copies = []
-    for n, (dy, dx) in enumerate(AROUND):
-        if dx == 0:
-            source, target = tile_ref, rows_in.at[0 if dy == 1 else 1]
-        else:
-            source, target = strips.at[0 if dx == -1 else 1], sides_in.at[1 - dy, 0 if dx == 1 else 1]
-        copies.append(
-            pltpu.make_async_remote_copy(
-                src_ref=source,
-                dst_ref=target,
-                send_sem=send_sem.at[n],
-                recv_sem=recv_sem.at[n],
-                device_id=device(dy, dx),
-                device_id_type=MESH,
-            )
-        )
-        pl.when(inside(dy, dx))(copies[-1].start)
-
     for load in loads[1:]:
         load.wait()
     build_conv_weights(second, near2, far2)
@@ -183,6 +162,27 @@
         wh[py * C : py * C + C, :] = jnp.dot(
             head_ref[...], columns_ref[py], preferred_element_type=F32
         ).astype(BF)
+
+    beside_y = 2 - at_low_y.astype(jnp.int32) - at_high_y.astype(jnp.int32)
+    beside_x = 2 - at_low_x.astype(jnp.int32) - at_high_x.astype(jnp.int32)
+    pl.semaphore_wait(barrier, (beside_y + 1) * (beside_x + 1) - 1)
+    copies = []
+    for n, (dy, dx) in enumerate(AROUND):
+        if dx == 0:
+            source, target = tile_ref, rows_in.at[0 if dy == 1 else 1]
+        else:
+            source, target = strips.at[0 if dx == -1 else 1], sides_in.at[1 - dy, 0 if dx == 1 else 1]
+        copies.append(
+            pltpu.make_async_remote_copy(
+                src_ref=source,
+                dst_ref=target,
+                send_sem=send_sem.at[n],
+                recv_sem=recv_sem.at[n],
+                device_id=device(dy, dx),
+                device_id_type=MESH,
+            )
+        )
+        pl.when(inside(dy, dx))(copies[-1].start)
 
     lane8 = lax.broadcasted_iota(jnp.int32, (TY, TX), 1)
     lane128 = lax.broadcasted_iota(jnp.int32, (Z * TY, TX), 1)

time: 27.3 us -> 27.3 us (level)
  no operation moved by 1% of the time
where the time goes in v9:
time: 27.3 us; the launch traced here: 27.2 us
  Pallas kernels  26.5 us (97%)
  local copies, waits for them, and re-layouts  0.68 us (2%)
    pallas_call x1, Pallas kernels, local(): pl.pallas_call(compute_kernel, out_shape=pltpu.VMEM((3, Z, TY, TX), F32),...  26.5 us
    unnamed x1, local copies, waits for them, and re-layouts  0.68 us

profile of v9, /device:TPU:1, one launch (start us, length us, event | category | flops | bytes accessed | tf_op | source)
XLA Modules:
  0.0 27.2 jit_solution(13916442763853230797)
XLA Ops:
  0.0 26.5 %convnet.1 = f32[3,16,8,128]{3,2,1,0:T(8,128)S(1)} custom-call(bf16[16,8,128]{2,1,0:T(8,128)(2,1)} %tile_hbm.1, bf16[6,256,128]{2,1,0:T(8,128)(2,1)} %constant.6.clone.place_hbm, bf16[9,3,64]{2,1,0:T(4,128)(2,1)} %bitcast.5, bf16[27,64,64]{2,1,0:T(8,128)(2,1)} %bitcast.3, bf16[27,64,64]{2,1,0:T(8,128)(2,1)} %bitcast.4, bf16[64,75]{1,0:T(8,128)(2,1)} %head_hbm.1, ...), custom_call_target="tpu_custom_call" | custom-call | tf_op jit(solution)/shard_map/convnet/pallas_call | solution.py:462
  26.5 0.7 %copy.10 = f32[3,16,8,128]{3,2,1,0:T(8,128)} copy(f32[3,16,8,128]{3,2,1,0:T(8,128)S(1)} %convnet.1) | data formatting | bytes 393216

commit v10 on v9

--- a/solution.py
+++ b/solution.py
@@ -197,7 +197,8 @@
         parts = []
         for half in range(2):
             parts += [buffer[half, z], buffer[half, z + 1], buffer[half, z + 2], filler]
-        return jnp.concatenate(parts, axis=0).T
+        whole = jnp.concatenate(parts, axis=0)
+        return (whole if buffer is main else whole[:, :24]).T
 
     own = tile_ref[...].astype(F32)
     main[0, 1 : Z + 1, 0:TY, :] = own
@@ -276,13 +277,13 @@
         rows = slice(part * TY, part * TY + TY)
         main[0, 1 : Z + 1, rows, :] = middle
         main[1, 1 : Z + 1, rows, :] = jnp.where(end, next_sides, next_middle)
-        edge[0, 1 : Z + 1, rows, :] = sides
-        edge[1, 1 : Z + 1, rows, :] = jnp.where(end, next_middle, next_sides)
+        edge[0, 1 : Z + 1, rows, :] = pltpu.roll(sides, 16, axis=2)
+        edge[1, 1 : Z + 1, rows, :] = pltpu.roll(jnp.where(end, next_middle, next_sides), 16, axis=2)
     for z in range(Z):
         sides = turn(edge, z)
         qf[pl.ds(8 * Z + z, TX, stride=Z), :] = turn(main, z)
-        qf[pl.ds(z, 8, stride=Z), :] = sides[120:128]
-        qf[pl.ds(136 * Z + z, 8, stride=Z), :] = sides[0:8]
+        qf[pl.ds(z, 8, stride=Z), :] = sides[8:16]
+        qf[pl.ds(136 * Z + z, 8, stride=Z), :] = sides[16:24]
     for m in range(STEM_X + 1):
         qb[m] = qf[(2 * m + 3) * Z : (2 * m + 4) * Z, :].astype(BF)
 

time: 27.3 us -> 27.4 us (level)
  no operation moved by 1% of the time
where the time goes in v10:
time: 27.4 us; the launch traced here: 27.2 us
  Pallas kernels  26.5 us (97%)
  local copies, waits for them, and re-layouts  0.68 us (2%)
    pallas_call x1, Pallas kernels, local(): pl.pallas_call(compute_kernel, out_shape=pltpu.VMEM((3, Z, TY, TX), F32),...  26.5 us
    unnamed x1, local copies, waits for them, and re-layouts  0.68 us

profile of v10, /device:TPU:1, one launch (start us, length us, event | category | flops | bytes accessed | tf_op | source)
XLA Modules:
  0.0 27.2 jit_solution(9191384006596121606)
XLA Ops:
  0.0 26.5 %convnet.1 = f32[3,16,8,128]{3,2,1,0:T(8,128)S(1)} custom-call(bf16[16,8,128]{2,1,0:T(8,128)(2,1)} %tile_hbm.1, bf16[6,256,128]{2,1,0:T(8,128)(2,1)} %constant.6.clone.place_hbm, bf16[9,3,64]{2,1,0:T(4,128)(2,1)} %bitcast.5, bf16[27,64,64]{2,1,0:T(8,128)(2,1)} %bitcast.3, bf16[27,64,64]{2,1,0:T(8,128)(2,1)} %bitcast.4, bf16[64,75]{1,0:T(8,128)(2,1)} %head_hbm.1, ...), custom_call_target="tpu_custom_call" | custom-call | tf_op jit(solution)/shard_map/convnet/pallas_call | solution.py:463
  26.5 0.7 %copy.10 = f32[3,16,8,128]{3,2,1,0:T(8,128)} copy(f32[3,16,8,128]{3,2,1,0:T(8,128)S(1)} %convnet.1) | data formatting | bytes 393216
